TPU v7x, 32 devices: a whole 2x2x4 slice. The times are simulated.
32 devices in a mesh: seq: 8 (over z, x), dp: 4 (over y, core).
Axes of the slice: x: 2, y: 2, z: 4, core: 2. Of those that a mesh axis runs over, the one named last changes fastest.
Arguments:
- tokens: bfloat16 [4, 2048, 1024], P('dp', 'seq'), may hold values from -6 to 6
- attn_gain: bfloat16 [1024], P(('seq', 'dp')), may hold values from 0.099609375 to 1.8984375
- query_weight: bfloat16 [1024, 256], P(('seq', 'dp')), may hold values from -0.1875 to 0.1875
- key_weight: bfloat16 [1024, 256], P(('seq', 'dp')), may hold values from -0.1875 to 0.1875
- value_weight: bfloat16 [1024, 1024], P(('seq', 'dp')), may hold values from -0.1875 to 0.1875
- out_weight: bfloat16 [1024, 1024], P(None, ('seq', 'dp')), may hold values from -3 to 3
- ffn_gain: bfloat16 [1024], P(('seq', 'dp')), may hold values from 0.099609375 to 1.8984375
- gate_weight: bfloat16 [1024, 2752], P(('seq', 'dp')), may hold values from -0.1875 to 0.1875
- up_weight: bfloat16 [1024, 2752], P(('seq', 'dp')), may hold values from -0.1875 to 0.1875
- down_weight: bfloat16 [2752, 1024], P(None, ('seq', 'dp')), may hold values from -0.109375 to 0.109375
- cotangent: bfloat16 [4, 2048, 1024], P('dp', 'seq'), may hold values from -6 to 6
Outputs:
- output: bfloat16 [4, 2048, 1024], P('dp', 'seq')
- input_grad: float32 [4, 2048, 1024], P('dp', 'seq')
- attn_gain_grad: float32 [1024], P(('seq', 'dp'))
- query_grad: float32 [1024, 256], P(('seq', 'dp'))
- key_grad: float32 [1024, 256], P(('seq', 'dp'))
- value_grad: float32 [1024, 1024], P(('seq', 'dp'))
- out_grad: float32 [1024, 1024], P(None, ('seq', 'dp'))
- ffn_gain_grad: float32 [1024], P(('seq', 'dp'))
- gate_grad: float32 [1024, 2752], P(('seq', 'dp'))
- up_grad: float32 [1024, 2752], P(('seq', 'dp'))
- down_grad: float32 [2752, 1024], P(None, ('seq', 'dp'))
All inputs are finite; a program needn't handle non-finite values.
Results may differ from a plain program's by a relative error of at most 0.017.
Values may be sent and summed in bfloat16 or wider, within the bound.
A program may use at most 320 MiB of HBM per device.

v0:
```python
import jax
import jax.numpy as jnp
from jax import lax
from jax.sharding import PartitionSpec as P

HEADS = 16
FDIM = 16
VDIM = 64
FEAT = 273
QK_WIDTH = 256
V_WIDTH = 1024


epsilon = 1e-05


def prefix_2(x, axis, join, neutral, backward):
    count = lax.axis_size(axis)
    place = lax.axis_index(axis)
    ahead = count - 1 - place if backward else place
    gathered = jax.tree.map(
        lambda a, kind: lax.all_gather(a.astype(kind), axis), x, (jnp.bfloat16, jnp.bfloat16)
    )
    state = jax.tree.map(lambda a, e: jnp.zeros_like(a) + jnp.asarray(e, a.dtype), x, neutral)

    def one(step, state):
        source = count - 1 - step if backward else step
        return join(
            state,
            jax.tree.map(
                lambda a, own: lax.dynamic_index_in_dim(a, source, 0, False).astype(own.dtype),
                gathered,
                x,
            ),
        )

    return lax.fori_loop(0, ahead, one, state)


def matmul(left, right):
    return jnp.dot(left, right, preferred_element_type=jnp.float32)


def left_inner(left, right):
    return lax.dot_general(
        left, right, (((0,), (0,)), ((), ())), preferred_element_type=jnp.float32
    )


def right_inner(left, right):
    return lax.dot_general(
        left, right, (((1,), (1,)), ((), ())), preferred_element_type=jnp.float32
    )


def taylor(vector):
    feature_dim = vector.shape[-1]
    leading = vector.shape[:-1]
    constant = jnp.ones(leading + (1,), vector.dtype)
    product = (vector[..., :, None] * vector[..., None, :]).reshape(
        leading + (feature_dim * feature_dim,)
    )
    return jnp.concatenate(
        [constant, vector * feature_dim ** (-0.25), product * (2.0 * feature_dim) ** (-0.5)],
        axis=-1,
    )


def norm_back(source, scale, gain, grad_normed):
    weighted = grad_normed * gain
    grad_gain = jnp.sum(grad_normed * source * scale, axis=0)
    cubed = scale * scale * scale
    grad_source = scale * weighted - source * cubed * jnp.mean(
        weighted * source, axis=-1, keepdims=True
    )
    return (grad_source, grad_gain)


def add_pair(earlier, later):
    return (earlier[0] + later[0], earlier[1] + later[1])


def split_columns(packed, widths):
    pieces = []
    offset = 0
    for width in widths:
        pieces.append(packed[:, offset : offset + width])
        offset = offset + width
    return pieces


def body(
    tokens,
    attn_gain,
    query_weight,
    key_weight,
    value_weight,
    out_weight,
    ffn_gain,
    gate_weight,
    up_weight,
    down_weight,
    cotangent,
):
    gathered = (
        lax.all_gather(attn_gain, ("seq", "dp"), axis=0, tiled=True),
        lax.all_gather(query_weight, ("seq", "dp"), axis=0, tiled=True),
        lax.all_gather(key_weight, ("seq", "dp"), axis=0, tiled=True),
        lax.all_gather(value_weight, ("seq", "dp"), axis=0, tiled=True),
        lax.all_gather(out_weight, ("seq", "dp"), axis=1, tiled=True),
        lax.all_gather(ffn_gain, ("seq", "dp"), axis=0, tiled=True),
        lax.all_gather(gate_weight, ("seq", "dp"), axis=0, tiled=True),
        lax.all_gather(up_weight, ("seq", "dp"), axis=0, tiled=True),
        lax.all_gather(down_weight, ("seq", "dp"), axis=1, tiled=True),
    )
    g_attn, w_query, w_key, w_value, w_out, g_ffn, w_gate, w_up, w_down = gathered
    seq_count, block_len, model_width = tokens.shape
    row_count = seq_count * block_len
    source = tokens.astype(jnp.float32).reshape(row_count, model_width)
    scale_one = lax.rsqrt(jnp.mean(source * source, axis=-1, keepdims=True) + epsilon)
    normed = (source * scale_one * g_attn.astype(jnp.float32)).astype(jnp.bfloat16)
    query = matmul(normed, w_query).reshape(row_count, HEADS, FDIM)
    keyvec = matmul(normed, w_key).reshape(row_count, HEADS, FDIM)
    values = matmul(normed, w_value).astype(jnp.bfloat16).reshape(seq_count, block_len, HEADS, VDIM)
    feat_q = taylor(query).astype(jnp.bfloat16).reshape(seq_count, block_len, HEADS, FEAT)
    feat_k = taylor(keyvec).astype(jnp.bfloat16).reshape(seq_count, block_len, HEADS, FEAT)
    units = jnp.einsum("sjhf,sjhd->shfd", feat_k, values, preferred_element_type=jnp.float32)
    counts = jnp.sum(feat_k, axis=1, dtype=jnp.float32)
    prefix, prior = prefix_2(
        (units, counts), "seq", add_pair, (jnp.zeros_like(units), jnp.zeros_like(counts)), False
    )
    prefix_low = prefix.astype(jnp.bfloat16)
    prior_low = prior.astype(jnp.bfloat16)
    scores = jnp.einsum(
        "sihf,sjhf->shij", feat_q, feat_k, preferred_element_type=jnp.float32
    ).astype(jnp.bfloat16)
    numer = jnp.einsum("shij,sjhd->sihd", scores, values, preferred_element_type=jnp.float32)
    numer = numer + jnp.einsum(
        "sihf,shfd->sihd", feat_q, prefix_low, preferred_element_type=jnp.float32
    )
    denom = jnp.transpose(jnp.sum(scores, axis=-1, dtype=jnp.float32), (0, 2, 1))
    denom = denom + jnp.einsum(
        "sihf,shf->sih", feat_q, prior_low, preferred_element_type=jnp.float32
    )
    attended = (numer / denom[..., None]).astype(jnp.bfloat16).reshape(row_count, V_WIDTH)
    middle = source + matmul(attended, w_out)
    scale_two = lax.rsqrt(jnp.mean(middle * middle, axis=-1, keepdims=True) + epsilon)
    normed_two = (middle * scale_two * g_ffn.astype(jnp.float32)).astype(jnp.bfloat16)
    gate = matmul(normed_two, w_gate)
    upper = matmul(normed_two, w_up)
    hidden = (jax.nn.silu(gate) * upper).astype(jnp.bfloat16)
    output = (
        (middle + matmul(hidden, w_down))
        .astype(jnp.bfloat16)
        .reshape(seq_count, block_len, model_width)
    )
    weights_again = (
        lax.all_gather(attn_gain, ("seq", "dp"), axis=0, tiled=True),
        lax.all_gather(query_weight, ("seq", "dp"), axis=0, tiled=True),
        lax.all_gather(key_weight, ("seq", "dp"), axis=0, tiled=True),
        lax.all_gather(value_weight, ("seq", "dp"), axis=0, tiled=True),
        lax.all_gather(out_weight, ("seq", "dp"), axis=1, tiled=True),
        lax.all_gather(ffn_gain, ("seq", "dp"), axis=0, tiled=True),
        lax.all_gather(gate_weight, ("seq", "dp"), axis=0, tiled=True),
        lax.all_gather(up_weight, ("seq", "dp"), axis=0, tiled=True),
        lax.all_gather(down_weight, ("seq", "dp"), axis=1, tiled=True),
    )
    g_attn, w_query, w_key, w_value, w_out, g_ffn, w_gate, w_up, w_down = weights_again
    ffn_width = w_gate.shape[1]
    grad_output = cotangent.reshape(row_count, model_width)
    grad_down_t = left_inner(grad_output, hidden)
    grad_hidden = right_inner(grad_output, w_down)
    sigmoid_gate = jax.nn.sigmoid(gate)
    grad_gate = (grad_hidden * upper * sigmoid_gate * (1.0 + gate * (1.0 - sigmoid_gate))).astype(
        jnp.bfloat16
    )
    grad_upper = (grad_hidden * (gate * sigmoid_gate)).astype(jnp.bfloat16)
    grad_gate_w = left_inner(normed_two, grad_gate)
    grad_up_w = left_inner(normed_two, grad_upper)
    grad_normed_two = right_inner(grad_gate, w_gate) + right_inner(grad_upper, w_up)
    grad_middle, grad_g_ffn = norm_back(
        middle, scale_two, g_ffn.astype(jnp.float32), grad_normed_two
    )
    grad_middle = grad_middle + grad_output.astype(jnp.float32)
    grad_mid_low = grad_middle.astype(jnp.bfloat16)
    grad_out_t = left_inner(grad_mid_low, attended)
    grad_att = right_inner(grad_mid_low, w_out).reshape(seq_count, block_len, HEADS, VDIM)
    ffn_widths = (1, V_WIDTH, ffn_width, ffn_width, ffn_width)
    grad_numer = (grad_att / denom[..., None]).astype(jnp.bfloat16)
    grad_denom = (-jnp.sum(grad_att * numer, axis=-1) / (denom * denom)).astype(jnp.bfloat16)
    scores_again = jnp.einsum(
        "sihf,sjhf->shij", feat_q, feat_k, preferred_element_type=jnp.float32
    ).astype(jnp.bfloat16)
    grad_scores = jnp.einsum(
        "sihd,sjhd->shij", grad_numer, values, preferred_element_type=jnp.float32
    )
    grad_scores = (
        grad_scores + jnp.transpose(grad_denom.astype(jnp.float32), (0, 2, 1))[..., None]
    ).astype(jnp.bfloat16)
    state_grad = jnp.einsum(
        "sihf,sihd->shfd", feat_q, grad_numer, preferred_element_type=jnp.float32
    )
    count_grad = jnp.einsum("sihf,sih->shf", feat_q, grad_denom, preferred_element_type=jnp.float32)
    later_state, later_count = prefix_2(
        (state_grad, count_grad),
        "seq",
        add_pair,
        (jnp.zeros_like(state_grad), jnp.zeros_like(count_grad)),
        True,
    )
    later_low = later_state.astype(jnp.bfloat16)
    grad_fq = jnp.einsum("shij,sjhf->sihf", grad_scores, feat_k, preferred_element_type=jnp.float32)
    grad_fq = grad_fq + jnp.einsum(
        "sihd,shfd->sihf", grad_numer, prefix_low, preferred_element_type=jnp.float32
    )
    grad_fq = grad_fq + jnp.einsum(
        "sih,shf->sihf", grad_denom, prior_low, preferred_element_type=jnp.float32
    )
    grad_fk = jnp.einsum("shij,sihf->sjhf", grad_scores, feat_q, preferred_element_type=jnp.float32)
    grad_fk = grad_fk + jnp.einsum(
        "sjhd,shfd->sjhf", values, later_low, preferred_element_type=jnp.float32
    )
    grad_fk = grad_fk + later_count[:, None]
    grad_values = jnp.einsum(
        "shij,sihd->sjhd", scores_again, grad_numer, preferred_element_type=jnp.float32
    )
    grad_values = grad_values + jnp.einsum(
        "sjhf,shfd->sjhd", feat_k, later_low, preferred_element_type=jnp.float32
    )
    grad_values = grad_values.astype(jnp.bfloat16).reshape(row_count, V_WIDTH)
    grad_query = jax.vjp(taylor, query)[1](grad_fq.reshape(row_count, HEADS, FEAT))[0]
    grad_query = grad_query.astype(jnp.bfloat16).reshape(row_count, QK_WIDTH)
    grad_keyvec = jax.vjp(taylor, keyvec)[1](grad_fk.reshape(row_count, HEADS, FEAT))[0]
    grad_keyvec = grad_keyvec.astype(jnp.bfloat16).reshape(row_count, QK_WIDTH)
    grad_query_w = left_inner(normed, grad_query)
    grad_key_w = left_inner(normed, grad_keyvec)
    grad_value_w = left_inner(normed, grad_values)
    grad_normed = (
        right_inner(grad_query, w_query)
        + right_inner(grad_keyvec, w_key)
        + right_inner(grad_values, w_value)
    )
    grad_source, grad_g_attn = norm_back(source, scale_one, g_attn.astype(jnp.float32), grad_normed)
    input_grad = (grad_middle + grad_source).reshape(seq_count, block_len, model_width)
    attn_widths = (1, QK_WIDTH, QK_WIDTH, V_WIDTH)
    all_packed = jnp.concatenate(
        [
            grad_g_attn[:, None],
            grad_query_w,
            grad_key_w,
            grad_value_w,
            grad_g_ffn[:, None],
            grad_out_t,
            grad_gate_w,
            grad_up_w,
            grad_down_t,
        ],
        axis=1,
    )
    all_parts = split_columns(
        lax.psum_scatter(all_packed, ("seq", "dp"), scatter_dimension=0, tiled=True),
        attn_widths + ffn_widths,
    )
    attn_parts = all_parts[:4]
    ffn_parts = all_parts[4:]
    return (
        output,
        input_grad,
        attn_parts[0][:, 0],
        attn_parts[1],
        attn_parts[2],
        attn_parts[3],
        jnp.transpose(ffn_parts[1]),
        ffn_parts[0][:, 0],
        ffn_parts[2],
        ffn_parts[3],
        jnp.transpose(ffn_parts[4]),
    )


def solution(mesh):
    return jax.shard_map(
        body,
        mesh=mesh,
        in_specs=(
            P("dp", "seq", None),
            P(("seq", "dp")),
            P(("seq", "dp"), None),
            P(("seq", "dp"), None),
            P(("seq", "dp"), None),
            P(None, ("seq", "dp")),
            P(("seq", "dp")),
            P(("seq", "dp"), None),
            P(("seq", "dp"), None),
            P(None, ("seq", "dp")),
            P("dp", "seq", None),
        ),
        out_specs=(
            P("dp", "seq", None),
            P("dp", "seq", None),
            P(("seq", "dp")),
            P(("seq", "dp"), None),
            P(("seq", "dp"), None),
            P(("seq", "dp"), None),
            P(None, ("seq", "dp")),
            P(("seq", "dp")),
            P(("seq", "dp"), None),
            P(("seq", "dp"), None),
            P(None, ("seq", "dp")),
        ),
        check_vma=False,
    )
```

profile of v0, /device:TPU:1, one launch (start us, length us, event | category | flops | bytes accessed | tf_op | source)
XLA Modules:
  0.0 1286.5 jit_solution(13832622088276867374)
XLA Ops:
  9.7 41.0 %all-reduce.2 = (bf16[1024]{0:T(1024)(128)(2,1)S(1)}, bf16[1024]{0:T(1024)(128)(2,1)S(1)}) all-reduce(bf16[1024]{0:T(1024)(128)(2,1)S(1)} %dynamic-update-slice, bf16[1024]{0:T(1024)(128)(2,1)S(1)} %dynamic-update-slice.1), channel_id=1, replica_groups=mesh['seq'=8,'dp'=4] {'seq','dp'}, use_global_device_ids=true, to_apply=%add | all-reduce | flops 2048 | bytes 8192
  50.7 43.2 %all_gather.63 = bf16[1024,256]{1,0:T(8,128)(2,1)S(1)} all-gather(bf16[32,256]{1,0:T(8,128)(2,1)} %param.18), channel_id=1, replica_groups=mesh['seq'=8,'dp'=4] {'seq','dp'}, dimensions={0}, use_global_device_ids=true | all-gather | bytes 540672 | tf_op jit(solution)/shard_map/all_gather | solution.py:108
  98.9 3.9 convolution_convert_fusion.3
  104.0 1.9 convolution_convert_fusion.2
  108.5 42.7 %all_gather.62 = bf16[1024,256]{1,0:T(8,128)(2,1)} all-gather(bf16[32,256]{1,0:T(8,128)(2,1)S(1)} %copy-done.51), channel_id=1, replica_groups=mesh['seq'=8,'dp'=4] {'seq','dp'}, dimensions={0}, use_global_device_ids=true | all-gather | bytes 540672 | tf_op jit(solution)/shard_map/all_gather | solution.py:107
  151.1 2.0 copy.66
  154.3 27.3 %all-gather.1 = bf16[128,273]{1,0:T(8,128)(2,1)} all-gather(bf16[16,273]{1,0:T(8,128)(2,1)S(1)} %maximum_reduce_fusion), channel_id=3, replica_groups=mesh['seq'=8,'dp'=4] {'seq'}, dimensions={0}, use_global_device_ids=true | all-gather | bytes 78624 | tf_op jit(solution)/shard_map/all_gather | solution.py:22
  183.8 2.5 convert_reduce_fusion
  189.1 15.2 %all-gather.22.cloned.1.call-done = bf16[128,273,64]{1,2,0:T(8,128)(2,1)} async-done(((bf16[16,273,64]{1,2,0:T(8,128)(2,1)}), bf16[128,273,64]{1,2,0:T(8,128)(2,1)}) %all-gather.22.cloned.1.call-update) | async-done | bytes 4472848 | tf_op jit(solution)/shard_map/all_gather | solution.py:22
  205.0 2.6 fusion.58
  207.6 2.1 divide_convert_fusion.1
  209.8 52.9 %all-gather.14.cloned.1.call-done = bf16[1024,1024]{0,1:T(8,128)(2,1)} async-done(((bf16[1024,32]{0,1:T(8,128)(2,1)}), bf16[1024,1024]{0,1:T(8,128)(2,1)}) %all-gather.14.cloned.1.call-update) | async-done | bytes 2097168 | tf_op jit(solution)/shard_map/all_gather | solution.py:110
  262.6 2.4 multiply_reduce_fusion.7
  266.3 65.3 %all-gather.18.cloned.1.call-done = bf16[1024,2752]{1,0:T(8,128)(2,1)} async-done(((bf16[32,2752]{1,0:T(8,128)(2,1)}), bf16[1024,2752]{1,0:T(8,128)(2,1)}) %all-gather.18.cloned.1.call-update) | async-done | bytes 5636112 | tf_op jit(solution)/shard_map/all_gather | solution.py:113
  331.5 6.6 fusion.76
  338.1 62.4 %all-gather.16.cloned.1.call-done = bf16[1024,2752]{1,0:T(8,128)(2,1)} async-done(((bf16[32,2752]{1,0:T(8,128)(2,1)}), bf16[1024,2752]{1,0:T(8,128)(2,1)}) %all-gather.16.cloned.1.call-update) | async-done | bytes 5636112 | tf_op jit(solution)/shard_map/all_gather | solution.py:112
  400.5 6.5 fusion.75
  407.1 62.5 %all-gather.20.cloned.1.call-done = bf16[2752,1024]{0,1:T(8,128)(2,1)} async-done(((bf16[2752,32]{0,1:T(8,128)(2,1)}), bf16[2752,1024]{0,1:T(8,128)(2,1)}) %all-gather.20.cloned.1.call-update) | async-done | bytes 5636112 | tf_op jit(solution)/shard_map/all_gather | solution.py:114
  469.6 8.9 multiply_convert_fusion.2
  478.5 1.9 fusion.77
  480.5 4.6 multiply_reduce_fusion.4
  489.2 1.9 convolution_convert_fusion.1
  492.9 2.5 fusion.61
  495.4 27.1 %all-gather.3 = bf16[128,273]{1,0:T(8,128)(2,1)} all-gather(bf16[16,273]{1,0:T(8,128)(2,1)S(1)} %bitcast.275), channel_id=5, replica_groups=mesh['seq'=8,'dp'=4] {'seq'}, dimensions={0}, use_global_device_ids=true | all-gather | bytes 78624 | tf_op jit(solution)/shard_map/all_gather | solution.py:22
  527.0 2.2 multiply_reduce_fusion.3
  533.8 2.8 fusion.54
  536.6 3.0 fusion.70
  539.6 5.8 fusion.82
  545.4 5.8 fusion.81
  551.2 5.7 convolution_bitcast_fusion
  557.0 32.1 %all-gather.24.cloned.1.call-done = bf16[128,273,64]{1,2,0:T(8,128)(2,1)} async-done(((bf16[16,273,64]{1,2,0:T(8,128)(2,1)}), bf16[128,273,64]{1,2,0:T(8,128)(2,1)}) %all-gather.24.cloned.1.call-update) | async-done | bytes 4472848 | tf_op jit(solution)/shard_map/all_gather | solution.py:22
  589.2 34.4 %while.27 = (s32[]{:T(128)}, f32[1,16,273,64]{3,2,1,0:T(8,128)S(1)}, f32[1,16,273]{2,1,0:T(8,128)S(1)}, s32[]{:T(128)}, bf16[8,1,16,273,64]{3,4,2,0,1:T(8,128)(2...) while((s32[]{:T(128)}, f32[1,16,273,64]{3,2,1,0:T(8,128)S(1)}, ...), condition=%wide.region_11.12_spmd, body=%wide.region_10.11_spmd.sunk | while | flops 567846 | bytes 5075779 | solution.py:37
  590.0 2.1 constant_dynamic-slice_fusion.5
  594.9 2.1 constant_dynamic-slice_fusion.5
  599.7 2.1 constant_dynamic-slice_fusion.5
  604.6 2.1 constant_dynamic-slice_fusion.5
  609.5 2.1 constant_dynamic-slice_fusion.5
  614.4 2.1 constant_dynamic-slice_fusion.5
  619.2 2.1 constant_dynamic-slice_fusion.5
  623.6 3.0 fusion.10
  626.7 3.0 fusion.40
  632.8 2.2 multiply_reduce_fusion.1
  638.9 118.0 %concatenate.47 = f32[1024,10818]{0,1:T(8,128)} concatenate(f32[1024,1]{0,1:T(1,128)S(1)} %bitcast.277, f32[1024,256]{0,1:T(8,128)S(1)} %copy-done.27, f32[1024,256]{0,1:T(8,128)S(1)} %fusion.44, f32[1024,1024]{0,1:T(8,128)} %fusion.40, f32[1024,1]{0,1:T(1,128)S(1)} %bitcast.278, f32[1024,1024]{0,1:T(8,128)} %fusion.54, f32[1024,2752]{0,1:T(8,128)} %fusion.81, ...), dimensions={1} | concatenate | bytes 88621056 | tf_op jit(solution)/shard_map/concatenate | solution.py:246
  757.0 43.9 %copy.96 = f32[1024,10818]{1,0:T(8,128)} copy(f32[1024,10818]{0,1:T(8,128)} %concatenate.47) | data formatting | bytes 88621056
  802.1 5.8 fusion.11
  809.2 462.1 %reduce-scatter.4.cloned.1.call-done = f32[32,10818]{1,0:T(8,128)} async-done(((f32[1024,10818]{1,0:T(8,128)}), f32[32,10818]{1,0:T(8,128)}) %reduce-scatter.4.cloned.1.call-update) | async-done | bytes 1384720
  1274.9 1.8 slice_bitcast_fusion.1
  1276.7 2.5 slice_bitcast_fusion
  (205 shorter events, 66.3 us)
Async XLA Ops:
  7.2 91.7 %all-gather.12.cloned.1.call-start = ((), (), s32[]{:S(2)}) async-start(), calls=%async_computation.1 | async-start | bytes 2162688 | tf_op jit(solution)/shard_map/all_gather | solution.py:109
  7.9 196.4 %all-gather.22.cloned.1.call-start = ((), (), s32[]{:S(2)}) async-start(), calls=%async_computation.6 | async-start | bytes 7077888 | tf_op jit(solution)/shard_map/all_gather | solution.py:22
  93.9 3.6 copy-start.25
  93.9 5.0 copy-start.2
  97.5 86.3 %copy-start.44 = (bf16[256,16,16]{0,2,1:T(8,128)(2,1)}, bf16[256,16,16]{0,2,1:T(8,128)(2,1)S(1)}, u32[]{:S(2)}) copy-start(bf16[256,16,16]{0,2,1:T(8,128)(2,1)S(1)} %get-tuple-element.253) | copy-start | bytes 393220
  98.8 84.9 %copy-start = (bf16[256,16,16,16]{0,3,2,1:T(8,128)(2,1)}, bf16[256,16,16,16]{0,3,2,1:T(8,128)(2,1)S(1)}, u32[]{:S(2)}) copy-start(bf16[256,16,16,16]{0,3,2,1:T(8,128)(2,1)S(1)} %multiply_convert_fusion) | copy-start | bytes 6291460
  104.0 82.3 %copy-start.19 = (bf16[256,1024]{0,1:T(8,128)(2,1)}, bf16[256,1024]{0,1:T(8,128)(2,1)S(1)}, u32[]{:S(2)}) copy-start(bf16[256,1024]{0,1:T(8,128)(2,1)S(1)} %copy.65) | copy-start | bytes 1572868
  104.0 4.5 copy-start.51
  105.9 156.7 %all-gather.14.cloned.1.call-start = ((), (), s32[]{:S(2)}) async-start(), calls=%async_computation.2 | async-start | bytes 2162688 | tf_op jit(solution)/shard_map/all_gather | solution.py:110
  106.7 224.9 %all-gather.18.cloned.1.call-start = ((), (), s32[]{:S(2)}) async-start(), calls=%async_computation.4 | async-start | bytes 5947392 | tf_op jit(solution)/shard_map/all_gather | solution.py:113
  107.2 293.3 %all-gather.16.cloned.1.call-start = ((), (), s32[]{:S(2)}) async-start(), calls=%async_computation.3 | async-start | bytes 5947392 | tf_op jit(solution)/shard_map/all_gather | solution.py:112
  107.8 361.7 %all-gather.20.cloned.1.call-start = ((), (), s32[]{:S(2)}) async-start(), calls=%async_computation.5 | async-start | bytes 5947392 | tf_op jit(solution)/shard_map/all_gather | solution.py:114
  108.4 480.7 %all-gather.24.cloned.1.call-start = ((), (), s32[]{:S(2)}) async-start(), calls=%async_computation.7 | async-start | bytes 7077888 | tf_op jit(solution)/shard_map/all_gather | solution.py:22
  183.1 3.2 copy-start.47
  183.7 2.6 copy-start.12
  204.9 2.7 copy-start.13
  204.9 2.7 copy-start.46
  205.0 2.7 copy-start.48
  207.6 55.0 %copy-start.3 = (bf16[1,256,1024]{2,1,0:T(8,128)(2,1)S(1)}, bf16[1,256,1024]{2,1,0:T(8,128)(2,1)}, u32[]{:S(2)}) copy-start(bf16[1,256,1024]{2,1,0:T(8,128)(2,1)} %param.15) | copy-start | bytes 1572868
  209.8 55.4 %copy-start.37 = (bf16[1,256,16,64]{1,3,2,0:T(8,128)(2,1)}, bf16[1,256,16,64]{1,3,2,0:T(8,128)(2,1)S(1)}, u32[]{:S(2)}) copy-start(bf16[1,256,16,64]{1,3,2,0:T(8,128)(2,1)S(1)} %get-tuple-element.259) | copy-start | bytes 1572868
  266.3 134.3 %copy-start.22 = (bf16[256,1024]{1,0:T(8,128)(2,1)}, bf16[256,1024]{1,0:T(8,128)(2,1)S(1)}, u32[]{:S(2)}) copy-start(bf16[256,1024]{1,0:T(8,128)(2,1)S(1)} %multiply_convert_fusion.5) | copy-start | bytes 1572868
  469.5 8.9 copy-start.53
  480.5 4.6 copy-start.35
  487.1 2.1 copy-start.49
  491.1 780.2 %reduce-scatter.4.cloned.1.call-start = ((), (), s32[]{:S(2)}) async-start(), calls=%async_computation.8 | async-start | bytes 45957120
  492.9 29.6 %copy-start.20 = (bf16[256,1024]{0,1:T(8,128)(2,1)S(1)}, bf16[256,1024]{0,1:T(8,128)(2,1)}, u32[]{:S(2)}) copy-start(bf16[256,1024]{0,1:T(8,128)(2,1)} %copy-done.19) | copy-start | bytes 1572868
  495.4 28.2 %copy-start.1 = (bf16[256,16,16,16]{0,3,2,1:T(8,128)(2,1)S(1)}, bf16[256,16,16,16]{0,3,2,1:T(8,128)(2,1)}, u32[]{:S(2)}) copy-start(bf16[256,16,16,16]{0,3,2,1:T(8,128)(2,1)} %copy-done) | copy-start | bytes 6291460
  495.4 28.2 %copy-start.45 = (bf16[256,16,16]{0,2,1:T(8,128)(2,1)S(1)}, bf16[256,16,16]{0,2,1:T(8,128)(2,1)}, u32[]{:S(2)}) copy-start(bf16[256,16,16]{0,2,1:T(8,128)(2,1)} %copy-done.44) | copy-start | bytes 393220
  527.0 2.3 copy-start.24
  529.2 2.8 copy-start.17
  530.6 3.1 copy-start.6
  530.6 3.1 copy-start.38
  533.8 2.8 copy-start.15
  533.8 2.8 copy-start.50
  536.6 3.0 copy-start.23
  536.6 3.0 copy-start.43
  539.6 5.8 copy-start.41
  545.4 5.8 copy-start.36
  545.4 5.8 copy-start.39
  623.6 3.0 copy-start.4
  626.7 3.1 slice-start
  626.7 3.5 slice-start.1
  626.7 3.9 copy-start.21
  635.1 2.3 copy-start.26
  635.1 2.3 copy-start.33
  802.1 5.8 copy-start.7
  802.1 5.8 copy-start.32
  802.1 5.8 copy-start.52
  (16 other events, 22.0 us)
Sparse Core Ops, SparseCore 0:
  10.9 59.6 all-gather.11
  106.0 98.2 all-gather.21
  207.2 55.4 all-gather.13
  265.4 66.1 all-gather.17
  334.3 66.2 all-gather.15
  403.3 66.2 all-gather.19
  491.2 97.7 all-gather.23
  801.0 470.2 reduce-scatter.3
where the time goes:
time: 1300 us; the launch traced here: 1290 us
  waiting for transfers between devices  756 us (58%)
  local copies, waits for them, and re-layouts  211 us (16%)
  blocking collectives  181 us (14%)
  matrix products  100 us (8%)
  other arithmetic  21.3 us (2%)
  between operations  15.3 us (1%)
    unnamed x9, waiting for transfers between devices  465 us
    concatenate x1, local copies, waits for them, and re-layouts, body(): jnp.concatenate([grad_g_attn[:, None], grad_query_w, grad_key_w, grad_val...  118 us
    all_gather x1, waiting for transfers between devices, body(): lax.all_gather(up_weight, ('seq', 'dp'), axis=0, tiled=True)  65.3 us
    all_gather x1, waiting for transfers between devices, body(): lax.all_gather(down_weight, ('seq', 'dp'), axis=1, tiled=True)  62.5 us
    all_gather x1, waiting for transfers between devices, body(): lax.all_gather(gate_weight, ('seq', 'dp'), axis=0, tiled=True)  62.4 us
    unnamed x119, local copies, waits for them, and re-layouts  56.5 us
    all_gather x2, blocking collectives, prefix_2(): lax.all_gather(a.astype(kind), axis)  54.4 us
    all_gather x1, waiting for transfers between devices, body(): lax.all_gather(out_weight, ('seq', 'dp'), axis=1, tiled=True)  52.9 us
  transfers between devices with their start and end apart: 8, of which 7 were waited for; matrix products, arithmetic and copies ran while one was open for 6% of the time, Pallas kernels for 0%

commit v1 on v0

v1 whole, which is shorter than its diff:
```python
import jax
import jax.numpy as jnp
from jax import lax
from jax.experimental import pallas as pl
from jax.experimental.pallas import tpu as pltpu
from jax.sharding import PartitionSpec as P

HEADS = 16
FDIM = 16
VDIM = 64
EPS = 1e-05
LIN = FDIM**-0.25
QUAD = (2.0 * FDIM) ** -0.5
SHIFTS = FDIM // 2 + 1
FEATS = FDIM * (SHIFTS + 2)
HALF_HEADS = HEADS // 2
QH = HALF_HEADS * FDIM
VH = HALF_HEADS * VDIM
PAIRS = HALF_HEADS // 2
SLOTS = 2 * PAIRS + 1
LANES = 128
PIECE = 512
RING = 6
MESH = pl.DeviceIdType.MESH
F32 = jnp.float32
BF16 = jnp.bfloat16


def pieces_of(width):
    out, at = [], 0
    while at < width:
        out.append((at, min(PIECE, width - at)))
        at += PIECE
    return out


def tiles_of(width):
    out, at = [], 0
    while at < width:
        out.append((at, min(256, width - at)))
        at += 256
    return out


def nn(a, b):
    return jnp.dot(a, b, preferred_element_type=F32)


def nt(a, b):
    return lax.dot_general(a, b, (((1,), (1,)), ((), ())), preferred_element_type=F32)


def tn(a, b):
    return lax.dot_general(a, b, (((0,), (0,)), ((), ())), preferred_element_type=F32)


def ahead(t, d):
    return t if d == 0 else pltpu.roll(t, FDIM - d, 0)


def behind(t, d):
    return t if d == 0 else pltpu.roll(t, d, 0)


def times(d):
    return 1.0 if d in (0, FDIM // 2) else 2.0


def features(u):
    rows = [u * ahead(u, d) * QUAD for d in range(SHIFTS)]
    first = lax.broadcasted_iota(jnp.int32, u.shape, 0) == 0
    rows += [u * LIN, jnp.where(first, 1.0, 0.0)]
    return jnp.concatenate(rows, axis=0).astype(BF16)


def weighted(f):
    lo, hi = FDIM, FDIM * (SHIFTS - 1)
    return jnp.concatenate([f[:lo], f[lo:hi] * 2, f[hi:]], axis=0)


def features_back(u, df):
    at = FDIM * SHIFTS
    total = df[at : at + FDIM] * LIN
    for d in range(SHIFTS):
        t = df[FDIM * d : FDIM * (d + 1)] * (QUAD * times(d))
        total = total + t * ahead(u, d) + behind(t * u, d)
    return total


def split_low(u):
    high = u.astype(BF16)
    return high, (u - high.astype(F32)).astype(BF16)


def plan(ff_half):
    parts = pieces_of(ff_half)
    gather = [("gain", LANES), ("qkv", 2 * QH + VH), ("out", VH)]
    gather += [(f"gu{j}", 2 * w) for j, (_, w) in enumerate(parts)]
    gather += [(f"d{j}", w) for j, (_, w) in enumerate(parts)]
    reduce = [(f"d{j}", w) for j, (_, w) in enumerate(parts)]
    for j, (_, w) in enumerate(parts):
        reduce += [(f"g{j}", w), (f"u{j}", w)]
    reduce += [("out", VH), ("qk", 2 * QH), ("v", VH), ("gain", LANES)]
    return gather, reduce


def make_kernel(seq_size, block, width, ff_half):
    gather, reduce = plan(ff_half)
    parts = pieces_of(ff_half)
    n_parts = len(parts)
    gi = {name: i for i, (name, _) in enumerate(gather)}
    ri = {name: i for i, (name, _) in enumerate(reduce)}
    members = seq_size // 8
    n_hi = seq_size // 2
    rows = width // 32
    rows2 = 2 * rows
    quarter = width // 4
    offsets = []
    total_width = 0
    for _, w in reduce:
        offsets.append(total_width)
        total_width += w
    n_hops = 4

    def kernel(*refs):
        it = iter(refs)
        take = lambda n: [next(it) for _ in range(n)]
        tok, cot = take(2)
        wp = take(len(gather))
        out_ref, din_ref = take(2)
        go = take(len(reduce))
        W = take(len(gather))
        G = take(len(reduce))
        (R1, R2, R3, FS, X, DY, NB, N1T, N2T, DYT, HID, CA, CB, X1, SND, RCV, OWN) = take(17)
        (NUM, DATT, QK, VT, ATT, DEN, DNUM, DDEN, DQK, DV, DQKV) = take(11)
        (ST, STXS, STSS, STO, PB, PX, WACC, TG, TU, GROW, GACC) = take(11)
        ss, rs, ls, bar2 = take(4)
        del bar2

        s, dp = lax.axis_index("seq"), lax.axis_index("dp")
        hi, x = s // 2, lax.rem(s, 2)
        y, c = dp // 2, lax.rem(dp, 2)
        g, m = hi // members, lax.rem(hi, members)
        o = 1 - c
        ax, ay = x + o * (1 - 2 * x), y + c * (1 - 2 * y)
        bx, by = x + c * (1 - 2 * x), y + o * (1 - 2 * y)
        p, pa = 2 * x + y, 2 * ax + ay
        pb, pab = 2 * bx + by, 2 * (1 - x) + (1 - y)

        def dev(hi_, x_, y_, c_):
            return (hi_ * 2 + x_, y_ * 2 + c_)

        partner = dev(hi, x, y, o)
        dev_a, dev_b = dev(hi, ax, ay, c), dev(hi, bx, by, c)
        dev_x = dev(hi, 1 - x, y, c)
        ups = [lax.rem(g + j, 4) for j in range(4)]
        downs = [lax.rem(g + 4 - j, 4) for j in range(4)]
        dev_up = [dev(u * members + m, x, y, c) for u in ups]
        right = dev(jnp.minimum(hi + 1, n_hi - 1), x, y, c)
        left = dev(jnp.maximum(hi - 1, 0), x, y, c)

        barrier = pltpu.get_barrier_semaphore()
        greet = [partner, dev_a, dev_b] + dev_up[1:]
        for d in greet:
            pl.semaphore_signal(barrier, inc=1, device_id=d, device_id_type=MESH)
        if members > 1:

            @pl.when(hi < n_hi - 1)
            def _():
                pl.semaphore_signal(barrier, inc=1, device_id=right, device_id_type=MESH)

            @pl.when(hi > 0)
            def _():
                pl.semaphore_signal(barrier, inc=1, device_id=left, device_id_type=MESH)

        pl.semaphore_wait(barrier, len(greet))
        if members > 1:

            @pl.when(hi < n_hi - 1)
            def _():
                pl.semaphore_wait(barrier, 1)

            @pl.when(hi > 0)
            def _():
                pl.semaphore_wait(barrier, 1)

        numbers = {}
        pending = []

        def number(key):
            return numbers.setdefault(key, len(numbers))

        def remote(key, src, dst, to):
            i = number(key)
            return pltpu.make_async_remote_copy(
                src_ref=src, dst_ref=dst, send_sem=ss.at[i], recv_sem=rs.at[i], device_id=to, device_id_type=MESH
            )

        def send(key, src, dst, to):
            d = remote(key, src, dst, to)
            d.start()
            pending.append((key, d))

        def sent(key):
            for k, d in list(pending):
                if k == key:
                    d.wait_send()
                    pending.remove((k, d))

        def got(key, ref):
            remote(key, ref, ref, partner).wait_recv()

        n_local = [0]
        local_pending = []

        def local(src, dst):
            d = pltpu.make_async_copy(src, dst, ls.at[n_local[0]])
            n_local[0] += 1
            d.start()
            return d

        started = {}

        def e0(i):
            r = wp[i].shape[1]
            mine = W[i].at[g, p, pl.ds(r * c, r)]
            started[i] = local(wp[i].at[c], mine)
            send(("e0", i), wp[i].at[o], mine, partner)

        def e1(i):
            r = wp[i].shape[1]
            started[i].wait()
            got(("e0", i), W[i].at[g, p, pl.ds(r * o, r)])
            for j in (1, 2, 3):
                send(("e1", i, j), W[i].at[g, p], W[i].at[g, p], dev_up[j])

        def e2(i):
            for j in (1, 2, 3):
                got(("e1", i, j), W[i].at[downs[j], p])
            send(("e2b", i), W[i].at[:, p], W[i].at[:, p], dev_b)
            send(("e2a", i), W[i].at[:, p], W[i].at[:, p], dev_a)

        def e3(i):
            got(("e2a", i), W[i].at[:, pa])
            send(("e3", i), W[i].at[:, pa], W[i].at[:, pa], dev_b)

        def e4(i):
            got(("e2b", i), W[i].at[:, pb])
            got(("e3", i), W[i].at[:, pab])

        done = {1: -1, 2: -1, 3: -1, 4: -1}

        def f1(i):
            w = reduce[i][1]
            k = i % RING
            for n, col in ((0, pab), (1, pb)):
                send(("f1", i, n), G[i].at[:, col], R1.at[k, n, :, :, 0:w], dev_b)

        def f2(i):
            w = reduce[i][1]
            k = i % RING
            got(("f1", i, 0), R1.at[k, 0, :, :, 0:w])
            G[i][:, pa] = G[i][:, pa] + R1[k, 0, :, :, 0:w]
            send(("f2", i), G[i].at[:, pa], R2.at[k, :, :, 0:w], dev_a)
            got(("f1", i, 1), R1.at[k, 1, :, :, 0:w])
            G[i][:, p] = G[i][:, p] + R1[k, 1, :, :, 0:w]

        def f3(i):
            w = reduce[i][1]
            k = i % RING
            got(("f2", i), R2.at[k, :, :, 0:w])
            G[i][:, p] = G[i][:, p] + R2[k, :, :, 0:w]
            for j in (1, 2, 3):
                send(("f3", i, j), G[i].at[ups[j], p], R3.at[k, j - 1, :, 0:w], dev_up[j])

        def f4(i):
            w, at = reduce[i][1], offsets[i]
            k = i % RING
            total = G[i][g, p].astype(F32)
            for j in (1, 2, 3):
                got(("f3", i, j), R3.at[k, j - 1, :, 0:w])
                total = total + R3[k, j - 1, :, 0:w].astype(F32)
            FS[:, :, at : at + w] = total.reshape(2, rows, w)
            local_pending.append(local(FS.at[c, :, at : at + w], go[i].at[c]))
            send(("f4", i), FS.at[o, :, at : at + w], go[i].at[c], partner)

        stages = {1: f1, 2: f2, 3: f3, 4: f4}

        def go_to(stage, last):
            while done[stage] < last:
                i = done[stage] + 1
                if stage < 4 and i >= RING // 2:
                    go_to(stage + 1, i - RING // 2)
                if stage > 1:
                    go_to(stage - 1, i)
                stages[stage](i)
                done[stage] = i

        def reduce_to(a, b=-1, cc=-1, dd=-1):
            if dd >= 0:
                go_to(4, dd)
            if cc >= 0:
                go_to(3, cc)
            if b >= 0:
                go_to(2, b)
            if a >= 0:
                go_to(1, a)

        def loop(n, body):
            def step(i, carry):
                body(i)
                return carry

            lax.fori_loop(0, n, step, 0)

        def put_grad(i, lhs_t, rhs):
            w = reduce[i][1]

            def one(k):
                a = lhs_t[pl.ds(pl.multiple_of(k * quarter, quarter), quarter), :]
                G[i][k] = nn(a, rhs()).astype(BF16).reshape(4, rows2, w)

            loop(4, one)

        def weight(i, at, w):
            return W[i][:, :, :, at : at + w].reshape(width, w)

        def transpose_in(src, dst, b):
            def one(k):
                at = pl.multiple_of(k * quarter, quarter)
                dst[pl.ds(at, quarter), pl.ds(pl.multiple_of(b * block, block), block)] = (
                    src[b, :, pl.ds(at, quarter)].astype(F32).T.astype(BF16)
                )

            loop(4, one)

        for i in range(len(gather)):
            e0(i)
        cx = local(tok, X.at[c])
        send("x", tok, X.at[c], partner)
        cy = local(cot, DY.at[c])
        send("dy", cot, DY.at[c], partner)
        e1(0)
        e1(1)
        e1(2)
        e1(3)
        cx.wait()
        cy.wait()
        got("x", X.at[o])
        got("dy", DY.at[o])
        e2(0)
        e2(1)
        e3(0)
        e1(4)
        transpose_in(DY, DYT, 0)
        transpose_in(DY, DYT, 1)
        e2(2)
        e4(0)
        e3(1)

        for k in range(8):
            kg, kx = k // 2, k % 2
            acc = None
            for ky in range(2):
                for kc in range(2):
                    t = W[0][kg, 2 * kx + ky, 16 * kc : 16 * kc + 16, :].astype(F32)
                    acc = t if acc is None else acc + t
            GROW[:, LANES * k : LANES * (k + 1)] = acc[:8]
        GACC[...] = jnp.zeros_like(GACC)

        step_rows = 16

        def norm_one(r):
            at = pl.multiple_of(r * step_rows, step_rows)
            for b in range(2):
                xs = X[b, pl.ds(at, step_rows), :].astype(F32)
                r1 = lax.rsqrt(jnp.mean(xs * xs, axis=-1, keepdims=True) + EPS)
                NB[b, pl.ds(at, step_rows), :] = (xs * r1 * GROW[0:1, :]).astype(BF16)

        loop(block // step_rows, norm_one)
        transpose_in(NB, N1T, 0)
        transpose_in(NB, N1T, 1)
        e2(3)
        e3(2)
        e1(5)
        e4(1)

        iq = gi["qkv"]
        both = NB[...].reshape(2 * block, width)
        t = nn(both, weight(iq, 0, 2 * QH))
        for b in range(2):
            QK[b] = t[block * b : block * (b + 1)].T
        for at, w in tiles_of(VH):
            t = nn(NB[...].reshape(2 * block, width), weight(iq, 2 * QH + at, w))
            for b in range(2):
                VT[b, at : at + w, :] = t[block * b : block * (b + 1)].T.astype(BF16)
        WACC[...] = jnp.zeros_like(WACC)
        lane = lax.broadcasted_iota(jnp.int32, (FEATS, LANES), 1)

        def place(i):
            b = i // PAIRS
            hp = lax.rem(i, PAIRS)
            return b, hp

        def q_rows(b, hp, e):
            return QK[b, pl.ds(pl.multiple_of(hp * 2 * FDIM + e * FDIM, FDIM), FDIM), :]

        def k_rows(b, hp, e):
            return QK[b, pl.ds(pl.multiple_of(QH + hp * 2 * FDIM + e * FDIM, FDIM), FDIM), :]

        def v_slice(hp):
            return pl.ds(pl.multiple_of(hp * 2 * VDIM, 2 * VDIM), 2 * VDIM)

        def head_slice(hp, e):
            return pl.ds(pl.multiple_of(hp * 2 * VDIM + e * VDIM, VDIM), VDIM)

        def put_state(i, f0, f1, right_side, w0, w1):
            low = nt(f0, right_side)
            high = nt(f1, right_side)
            ST[1 + i] = jnp.where(lane < VDIM, low, high).astype(BF16)
            WACC[...] += jnp.where(lane == 2 * i, w0, 0.0) + jnp.where(lane == 2 * i + 1, w1, 0.0)

        def state_step(i):
            b, hp = place(i)
            fs = [features(k_rows(b, hp, e)) for e in range(2)]
            ws = [jnp.sum(f.astype(F32), axis=1, keepdims=True) for f in fs]
            put_state(i, fs[0], fs[1], VT[b, v_slice(hp), :], ws[0], ws[1])

        loop(2 * PAIRS, state_step)
        ST[0] = WACC[...].astype(BF16)

        spans = ((0, PAIRS + 1), (PAIRS + 1, SLOTS))

        def state_exchange(n):
            for k, (lo, up) in enumerate(spans):
                send(("sx", n, k), ST.at[lo:up], STXS.at[n, lo:up], dev_x)

        def chain(n, hop, back):
            rank = n_hi - 1 - hi if back else hi
            to = left if back else right
            STX, STS = STXS.at[n], STSS.at[n]
            mine = rank == hop if hop < n_hops - 1 else rank >= hop

            @pl.when(mine)
            def _():
                for k, (lo, up) in enumerate(spans):
                    number(("sc", n, k))
                    d = remote(("sc", n, k), STO.at[lo:up], STS.at[lo:up], to)

                    if hop > 0:
                        got(("sc", n, k), STS.at[lo:up])
                    else:
                        STS[lo:up] = jnp.zeros((up - lo, FEATS, LANES), BF16)

                    @pl.when(rank < n_hi - 1)
                    def _():
                        def add(j):
                            STO[j] = (
                                STS[j].astype(F32) + (ST[j].astype(F32) + STX[j].astype(F32))
                            ).astype(BF16)

                        lax.fori_loop(lo, up, lambda j, z: (add(j), z)[1], 0)
                        d.start()

        def chain_sent(n, back):
            rank = n_hi - 1 - hi if back else hi

            @pl.when(rank < n_hi - 1)
            def _():
                for k, (lo, up) in enumerate(spans):
                    remote(("sc", n, k), STO.at[lo:up], STSS.at[n, lo:up], partner).wait_send()

        def chain_end(n, dst, near):
            def add(j):
                keep = jnp.where(near, STXS[n, j].astype(F32), 0.0)
                dst[j] = (STSS[n, j].astype(F32) + keep).astype(BF16)

            loop(SLOTS, add)

        def state_got(n):
            for k, (lo, up) in enumerate(spans):
                got(("sx", n, k), STXS.at[n, lo:up])

        state_exchange(0)
        e3(3)
        e2(4)
        e1(6)
        e4(2)
        state_got(0)
        chain(0, 0, False)
        e2(5)
        e3(4)
        e1(7)
        e4(3)
        chain(0, 1, False)
        e1(8)
        e2(6)
        e3(5)
        chain(0, 2, False)
        e2(7)
        e3(6)
        chain(0, 3, False)
        chain_end(0, PB, x == 1)

        def score_z(b, hp, e):
            qh, ql = split_low(q_rows(b, hp, e))
            kh, kl = split_low(k_rows(b, hp, e))
            return tn(jnp.concatenate([kh, kh, kl], axis=0), jnp.concatenate([qh, ql, qh], axis=0))

        def column(buf, at):
            return jnp.sum(jnp.where(lane == at, buf[0].astype(F32), 0.0), axis=1, keepdims=True)

        def att_step(i):
            b, hp = place(i)
            turned = PB[1 + i].astype(F32).T.astype(BF16)
            tops = []
            for e in range(2):
                z = score_z(b, hp, e)
                st = (1.0 + z * FDIM**-0.5 + z * z * (0.5 / FDIM)).astype(BF16)
                fq = weighted(features(q_rows(b, hp, e)))
                num = nn(VT[b, head_slice(hp, e), :], st) + nn(turned[VDIM * e : VDIM * (e + 1)], fq)
                den = jnp.sum(st.astype(F32), axis=0, keepdims=True) + jnp.sum(
                    fq.astype(F32) * column(PB, 2 * i + e), axis=0, keepdims=True
                )
                NUM[b, head_slice(hp, e), :] = num
                DEN[i, e : e + 1, :] = den
                tops.append(num / den)
            ATT[b, :, v_slice(hp)] = jnp.concatenate(tops, axis=0).T.astype(BF16)

        loop(2 * PAIRS, att_step)
        e2(8)
        e3(7)

        io = gi["out"]

        def col(k):
            return pl.ds(pl.multiple_of(k * quarter, quarter), quarter)

        def wrow(i, k, at, w):
            return W[i][k, :, :, at : at + w].reshape(quarter, w)

        def out_proj(dst, b):
            def one(k):
                dst[:, col(k)] = nt(ATT[b], wrow(io, k, 0, VH))

            loop(4, one)

        out_proj(SND.at[0], o)
        send("x1", SND.at[0], RCV.at[0], partner)
        out_proj(OWN, c)
        got("x1", RCV.at[0])

        def norm_two(r):
            at = pl.multiple_of(r * step_rows, step_rows)
            rr = pl.ds(at, step_rows)
            x1 = X[c, rr, :].astype(F32) + (OWN[rr, :] + RCV[0, rr, :])
            X1[rr, :] = x1
            r2 = lax.rsqrt(jnp.mean(x1 * x1, axis=-1, keepdims=True) + EPS)
            NB[c, rr, :] = (x1 * r2 * GROW[1:2, :]).astype(BF16)

        loop(block // step_rows, norm_two)
        send("n2", NB.at[c], NB.at[c], partner)
        transpose_in(NB, N2T, c)
        got("n2", NB.at[o])
        transpose_in(NB, N2T, o)

        def ffn_in(j):
            base, w = parts[j]
            i = gi[f"gu{j}"]
            for at, tw in tiles_of(w):
                TG[:, 0:tw] = nn(NB[...].reshape(2 * block, width), weight(i, at, tw))
                TU[:, 0:tw] = nn(NB[...].reshape(2 * block, width), weight(i, w + at, tw))
                lo = base + at

                def one(r):
                    rr = pl.ds(pl.multiple_of(r * 64, 64), 64)
                    gate, up = TG[rr, 0:tw], TU[rr, 0:tw]
                    sg = 1.0 / (1.0 + jnp.exp(-gate))
                    silu = gate * sg
                    HID[rr, lo : lo + tw] = (silu * up).astype(BF16)
                    CA[rr, lo : lo + tw] = (up * sg * (1.0 + gate * (1.0 - sg))).astype(BF16)
                    CB[rr, lo : lo + tw] = silu.astype(BF16)

                loop(2 * block // 64, one)
            put_grad(ri[f"d{j}"], DYT, lambda: HID[:, base : base + w])
            reduce_to(ri[f"d{j}"])

        for j in range(n_parts):
            if j:
                e4(gi[f"gu{j}"])
            ffn_in(j)
        e3(8)
        e4(6)
        e4(7)
        e4(8)

        def ffn_back(j):
            base, w = parts[j]
            i = gi[f"d{j}"]
            for at, tw in tiles_of(w):
                TG[:, 0:tw] = nn(DY[...].reshape(2 * block, width), weight(i, at, tw))
                lo = base + at

                def one(r):
                    rr = pl.ds(pl.multiple_of(r * 64, 64), 64)
                    dh = TG[rr, 0:tw]
                    CA[rr, lo : lo + tw] = (dh * CA[rr, lo : lo + tw].astype(F32)).astype(BF16)
                    CB[rr, lo : lo + tw] = (dh * CB[rr, lo : lo + tw].astype(F32)).astype(BF16)

                loop(2 * block // 64, one)

        for j in range(n_parts):
            ffn_back(j)
        reduce_to(-1, 0)

        def tokens_of(b):
            return pl.ds(pl.multiple_of(b * block, block), block)

        def dn2(dst, b):
            def one(k):
                acc = None
                for j, (base, w) in enumerate(parts):
                    i = gi[f"gu{j}"]
                    for buf, at in ((CA, 0), (CB, w)):
                        t = nt(buf[tokens_of(b), base : base + w], wrow(i, k, at, w))
                        acc = t if acc is None else acc + t
                dst[:, col(k)] = acc

            loop(4, one)

        sent("x1")
        dn2(SND.at[0], o)
        send("dn2", SND.at[0], RCV.at[1], partner)
        dn2(OWN, c)
        reduce_to(-1, 1, 0)
        put_grad(ri["g0"], N2T, lambda: CA[:, parts[0][0] : parts[0][0] + parts[0][1]])
        reduce_to(ri["g0"])
        got("dn2", RCV.at[1])
        sent("n2")

        def norm_two_back(r):
            at = pl.multiple_of(r * step_rows, step_rows)
            rr = pl.ds(at, step_rows)
            d = OWN[rr, :] + RCV[1, rr, :]
            x1 = X1[rr, :]
            r2 = lax.rsqrt(jnp.mean(x1 * x1, axis=-1, keepdims=True) + EPS)
            t = d * (x1 * r2)
            GACC[8:16, :] += t[:8] + t[8:]
            a2 = d * GROW[1:2, :]
            dx = DY[c, rr, :].astype(F32) + (
                r2 * a2 - x1 * (r2 * r2 * r2) * jnp.mean(a2 * x1, axis=-1, keepdims=True)
            )
            din_ref[rr, :] = dx
            NB[c, rr, :] = dx.astype(BF16)

        loop(block // step_rows, norm_two_back)
        send("dx1", NB.at[c], NB.at[c], partner)
        transpose_in(NB, DYT, c)
        put_grad(ri["u0"], N2T, lambda: CB[:, parts[0][0] : parts[0][0] + parts[0][1]])
        reduce_to(ri["u0"], 2)
        got("dx1", NB.at[o])
        transpose_in(NB, DYT, o)

        for at, tw in tiles_of(VH):
            t = nn(NB[...].reshape(2 * block, width), weight(io, at, tw))
            for b in range(2):
                DATT[b, at : at + tw, :] = t[block * b : block * (b + 1)].T
        WACC[...] = jnp.zeros_like(WACC)
        for k in range(len(spans)):
            sent(("sx", 0, k))
        chain_sent(0, False)

        def back_state_step(i):
            b, hp = place(i)
            fs, ws = [], []
            for e in range(2):
                hs = head_slice(hp, e)
                datt, num, den = DATT[b, hs, :], NUM[b, hs, :], DEN[i, e : e + 1, :]
                dd = (-jnp.sum(datt * num, axis=0, keepdims=True) / (den * den)).astype(BF16)
                DNUM[b, hs, :] = (datt / den).astype(BF16)
                DDEN[i, e : e + 1, :] = dd.astype(F32)
                f = features(q_rows(b, hp, e))
                fs.append(f)
                ws.append(jnp.sum(f.astype(F32) * dd.astype(F32), axis=1, keepdims=True))
            put_state(i, fs[0], fs[1], DNUM[b, v_slice(hp), :], ws[0], ws[1])

        loop(2 * PAIRS, back_state_step)
        ST[0] = WACC[...].astype(BF16)
        state_exchange(1)
        put_grad(ri["g1"], N2T, lambda: CA[:, parts[1][0] : parts[1][0] + parts[1][1]])
        reduce_to(ri["g1"], 3, 1)
        state_got(1)
        chain(1, 0, True)

        zeros_head = jnp.zeros((VDIM, block), BF16)

        def masked(t, e):
            return jnp.concatenate([zeros_head, t] if e else [t, zeros_head], axis=0)

        def back_step(i):
            b, hp = place(i)
            for e in range(2):
                hs = head_slice(hp, e)
                q, kk = q_rows(b, hp, e), k_rows(b, hp, e)
                qh, ql = split_low(q)
                kh, kl = split_low(kk)
                z = tn(jnp.concatenate([kh, kh, kl], axis=0), jnp.concatenate([qh, ql, qh], axis=0))
                st = (1.0 + z * FDIM**-0.5 + z * z * (0.5 / FDIM)).astype(BF16)
                dnum, dden = DNUM[b, hs, :], DDEN[i, e : e + 1, :]
                ds = (tn(VT[b, hs, :], dnum) + dden).astype(BF16).astype(F32)
                dz = (ds * (FDIM**-0.5 + z * (1.0 / FDIM))).astype(BF16)
                t = nn(jnp.concatenate([kh, kl], axis=0), dz)
                dq = t[:FDIM] + t[FDIM:]
                t = nt(jnp.concatenate([qh, ql], axis=0), dz)
                dk = t[:FDIM] + t[FDIM:]
                DV[b, hs, :] = nt(dnum, st)
                df = nn(PB[1 + i], masked(dnum, e)) + column(PB, 2 * i + e) * dden
                DQK[b, pl.ds(pl.multiple_of(hp * 2 * FDIM + e * FDIM, FDIM), FDIM), :] = dq + features_back(q, df)
                DQK[b, pl.ds(pl.multiple_of(QH + hp * 2 * FDIM + e * FDIM, FDIM), FDIM), :] = dk

        loop(2 * PAIRS, back_step)
        chain(1, 1, True)
        put_grad(ri["u1"], N2T, lambda: CB[:, parts[1][0] : parts[1][0] + parts[1][1]])
        reduce_to(ri["u1"], 4, 2)

        def y_part(dst, b):
            def one(k):
                acc = None
                for j, (base, w) in enumerate(parts):
                    t = nt(HID[tokens_of(b), base : base + w], wrow(gi[f"d{j}"], k, 0, w))
                    acc = t if acc is None else acc + t
                dst[:, col(k)] = acc

            loop(4, one)

        y_part(SND.at[1], o)
        send("y", SND.at[1], RCV.at[2], partner)
        y_part(OWN, c)
        chain(1, 2, True)
        for j in range(2, n_parts):
            put_grad(ri[f"g{j}"], N2T, lambda: CA[:, parts[j][0] : parts[j][0] + parts[j][1]])
            reduce_to(ri[f"g{j}"], ri[f"g{j}"] - 2, ri[f"g{j}"] - 4)
            put_grad(ri[f"u{j}"], N2T, lambda: CB[:, parts[j][0] : parts[j][0] + parts[j][1]])
        got("y", RCV.at[2])

        def finish(r):
            rr = pl.ds(pl.multiple_of(r * step_rows, step_rows), step_rows)
            out_ref[rr, :] = (X1[rr, :] + (OWN[rr, :] + RCV[2, rr, :])).astype(BF16)

        loop(block // step_rows, finish)
        chain(1, 3, True)
        chain_end(1, PX, x == 0)

        def key_step(i):
            b, hp = place(i)
            turned = PX[1 + i].astype(F32).T.astype(BF16)
            for e in range(2):
                hs = head_slice(hp, e)
                kk = k_rows(b, hp, e)
                df = nn(PX[1 + i], masked(VT[b, hs, :], e)) + column(PX, 2 * i + e)
                kr = pl.ds(pl.multiple_of(QH + hp * 2 * FDIM + e * FDIM, FDIM), FDIM)
                DQK[b, kr, :] += features_back(kk, df)
                DV[b, hs, :] += nn(turned[VDIM * e : VDIM * (e + 1)], weighted(features(kk)))

        loop(2 * PAIRS, key_step)
        for b in range(2):
            DQKV[b, :, 0 : 2 * QH] = DQK[b].T.astype(BF16)
            for at, tw in tiles_of(VH):
                DQKV[b, :, 2 * QH + at : 2 * QH + at + tw] = DV[b, at : at + tw, :].T.astype(BF16)

        def dn1(dst, b):
            def one(k):
                dst[:, col(k)] = nt(DQKV[b], wrow(iq, k, 0, 2 * QH + VH))

            loop(4, one)

        sent("dn2")
        dn1(SND.at[0], o)
        send("dn1", SND.at[0], RCV.at[0], partner)
        u_last = ri[f"u{n_parts - 1}"]
        reduce_to(u_last, u_last - 2, u_last - 4)
        put_grad(ri["out"], DYT, lambda: ATT[...].reshape(2 * block, VH))
        reduce_to(ri["out"], ri["out"] - 2, ri["out"] - 4)
        put_grad(ri["qk"], N1T, lambda: DQKV[:, :, 0 : 2 * QH].reshape(2 * block, 2 * QH))
        put_grad(ri["v"], N1T, lambda: DQKV[:, :, 2 * QH :].reshape(2 * block, VH))
        reduce_to(ri["qk"], ri["qk"] - 2, ri["qk"] - 4)
        dn1(OWN, c)
        got("dn1", RCV.at[0])

        def norm_one_back(r):
            rr = pl.ds(pl.multiple_of(r * step_rows, step_rows), step_rows)
            d = OWN[rr, :] + RCV[0, rr, :]
            xs = X[c, rr, :].astype(F32)
            r1 = lax.rsqrt(jnp.mean(xs * xs, axis=-1, keepdims=True) + EPS)
            t = d * (xs * r1)
            GACC[0:8, :] += t[:8] + t[8:]
            a1 = d * GROW[0:1, :]
            din_ref[rr, :] += r1 * a1 - xs * (r1 * r1 * r1) * jnp.mean(a1 * xs, axis=-1, keepdims=True)

        loop(block // step_rows, norm_one_back)
        ga = jnp.sum(GACC[0:8, :], axis=0, keepdims=True)
        gf = jnp.sum(GACC[8:16, :], axis=0, keepdims=True)
        last = ri["gain"]
        for k in range(4):
            row = lax.broadcasted_iota(jnp.int32, (LANES, quarter), 0)
            sl = slice(quarter * k, quarter * (k + 1))
            mat = jnp.where(row == 0, ga[:, sl], 0.0) + jnp.where(row == 1, gf[:, sl], 0.0)
            G[last][k] = mat.T.astype(BF16).reshape(4, rows2, LANES)
        n = len(reduce)
        reduce_to(n - 1, n - 3, n - 5)
        for k in range(n):
            go_to(2, min(n - 1, n - 3 + k))
            go_to(3, min(n - 1, n - 4 + k))
            go_to(4, min(n - 1, n - 5 + k))
        for i in range(n):
            got(("f4", i), go[i].at[o])
        for d in local_pending:
            d.wait()
        chain_sent(1, True)
        for _, d in pending:
            d.wait_send()

    return kernel


def call_kernel(tok, cot, packed, seq_size, ff_half):
    block, width = tok.shape
    gather, reduce = plan(ff_half)
    rows = width // 32
    quarter = width // 4
    vmem = pltpu.VMEM
    any_spec = pl.BlockSpec(memory_space=pl.ANY)
    total_width = sum(w for _, w in reduce)
    state = vmem((SLOTS, FEATS, LANES), BF16)
    scratch = [vmem((4, 4, 2 * a.shape[1], w), BF16) for a, (_, w) in zip(packed, gather)]
    scratch += [vmem((4, 4, 2 * rows, w), BF16) for _, w in reduce]
    scratch += [
        vmem((RING, 2, 4, 2 * rows, PIECE), BF16),
        vmem((RING, 4, 2 * rows, PIECE), BF16),
        vmem((RING, 3, 2 * rows, PIECE), BF16),
        vmem((2, rows, total_width), F32),
        vmem((2, block, width), BF16),
        vmem((2, block, width), BF16),
        vmem((2, block, width), BF16),
        vmem((width, 2 * block), BF16),
        vmem((width, 2 * block), BF16),
        vmem((width, 2 * block), BF16),
        vmem((2 * block, ff_half), BF16),
        vmem((2 * block, ff_half), BF16),
        vmem((2 * block, ff_half), BF16),
        vmem((block, width), F32),
        vmem((2, block, width), F32),
        vmem((3, block, width), F32),
        vmem((block, width), F32),
        vmem((2, VH, block), F32),
        vmem((2, VH, block), F32),
        vmem((2, 2 * QH, block), F32),
        vmem((2, VH, block), BF16),
        vmem((2, block, VH), BF16),
        vmem((2 * PAIRS, 8, block), F32),
        vmem((2, VH, block), BF16),
        vmem((2 * PAIRS, 8, block), F32),
        vmem((2, 2 * QH, block), F32),
        vmem((2, VH, block), F32),
        vmem((2, block, 2 * QH + VH), BF16),
        state,
        vmem((2, SLOTS, FEATS, LANES), BF16),
        vmem((2, SLOTS, FEATS, LANES), BF16),
        state,
        state,
        state,
        vmem((FEATS, LANES), F32),
        vmem((2 * block, 256), F32),
        vmem((2 * block, 256), F32),
        vmem((8, width), F32),
        vmem((16, width), F32),
        pltpu.SemaphoreType.DMA((256,)),
        pltpu.SemaphoreType.DMA((256,)),
        pltpu.SemaphoreType.DMA((64,)),
        pltpu.SemaphoreType.REGULAR,
    ]
    out_shape = [
        jax.ShapeDtypeStruct((block, width), BF16),
        jax.ShapeDtypeStruct((block, width), F32),
    ] + [jax.ShapeDtypeStruct((2, rows, w), F32) for _, w in reduce]
    return pl.pallas_call(
        make_kernel(seq_size, block, width, ff_half),
        out_shape=out_shape,
        in_specs=[any_spec] * (2 + len(packed)),
        out_specs=[pl.BlockSpec(memory_space=vmem)] * 2 + [any_spec] * len(reduce),
        scratch_shapes=scratch,
        compiler_params=pltpu.CompilerParams(
            collective_id=0, has_side_effects=True, vmem_limit_bytes=62 * 2**20
        ),
    )(tok, cot, *packed)


def body(
    tokens, attn_gain, query_weight, key_weight, value_weight, out_weight, ffn_gain, gate_weight, up_weight, down_weight, cotangent
):
    seq_size = lax.axis_size("seq")
    members = seq_size // 8
    _, block, width = tokens.shape
    ff = gate_weight.shape[1]
    ff_half = LANES * ((ff + 2 * LANES - 1) // (2 * LANES))
    few = attn_gain.shape[0]
    groups = [[(g * members + m) * 2 + x for m in range(members)] for g in range(4) for x in range(2)]

    def halves(w):
        return w.reshape(w.shape[0], 2, w.shape[1] // 2).transpose(1, 0, 2)

    def ff_halves(w):
        return halves(jnp.pad(w, ((0, 0), (0, 2 * ff_half - ff))))

    gates, ups, downs = ff_halves(gate_weight), ff_halves(up_weight), ff_halves(down_weight.T)
    parts = pieces_of(ff_half)
    packed = [jnp.concatenate([halves(query_weight), halves(key_weight), halves(value_weight)], axis=2), halves(out_weight.T)]
    packed += [jnp.concatenate([gates[:, :, a : a + w], ups[:, :, a : a + w]], axis=2) for a, w in parts]
    packed += [downs[:, :, a : a + w] for a, w in parts]
    gains = jnp.stack([attn_gain, ffn_gain])
    if members > 1:
        packed = [lax.all_gather(a, "seq", axis_index_groups=groups, axis=1, tiled=True) for a in packed]
        gains = lax.all_gather(gains, "seq", axis_index_groups=groups, axis=1, tiled=True)
    rows = members * few
    spot = lax.broadcasted_iota(jnp.int32, (2, 4 * rows), 1) // rows == lax.axis_index("dp")
    gain_rows = jnp.where(spot, jnp.tile(gains, (1, 4)), jnp.zeros((), BF16))
    gain_block = jnp.pad(gain_rows, ((0, 14), (0, 0)))
    packed = [jnp.stack([gain_block, gain_block])] + packed

    def turn(t):
        if members == 1:
            return t
        return t.reshape(block, 4, members, 2, 4, few).transpose(0, 1, 3, 4, 2, 5).reshape(block, width)

    def turn_back(t):
        if members == 1:
            return t
        return t.reshape(block, 4, 2, 4, members, few).transpose(0, 1, 4, 2, 3, 5).reshape(block, width)

    results = call_kernel(turn(tokens[0]), turn(cotangent[0]), packed, seq_size, ff_half)
    output, input_grad, grads = results[0], results[1], results[2:]
    if members > 1:
        grads = [
            lax.psum_scatter(a, "seq", scatter_dimension=1, axis_index_groups=groups, tiled=True) for a in grads
        ]
    _, reduce = plan(ff_half)
    by = {name: a for (name, _), a in zip(reduce, grads)}

    def joined(a):
        return jnp.concatenate([a[0], a[1]], axis=1)

    def ff_joined(letter):
        return joined(jnp.concatenate([by[f"{letter}{j}"] for j in range(len(parts))], axis=2))[:, :ff]

    gain = by["gain"][0] + by["gain"][1]
    return (
        turn_back(output)[None],
        turn_back(input_grad)[None],
        gain[:, 0],
        joined(by["qk"][:, :, :QH]),
        joined(by["qk"][:, :, QH:]),
        joined(by["v"]),
        joined(by["out"]).T,
        gain[:, 1],
        ff_joined("g"),
        ff_joined("u"),
        ff_joined("d").T,
    )


def solution(mesh):
    both = ("seq", "dp")
    row, column, whole = P(both, None), P(None, both), P("dp", "seq", None)
    return jax.shard_map(
        body,
        mesh=mesh,
        in_specs=(whole, P(both), row, row, row, column, P(both), row, row, column, whole),
        out_specs=(whole, whole, P(both), row, row, row, column, P(both), row, row, column),
        check_vma=False,
    )
```

time: 1300 us -> 283 us (0.22)
  waiting for transfers between devices: 756 us -> 0 us
  Pallas kernels: 0 us -> 260 us
  local copies, waits for them, and re-layouts: 211 us -> 14.2 us
  blocking collectives: 181 us -> 0 us
  matrix products: 100 us -> 0 us
  between operations: 15.3 us -> 0.91 us
  other arithmetic: 21.3 us -> 7.51 us
    unnamed x9 -> x0, waiting for transfers between devices: 465 us -> none
    all_gather x7 -> x0, waiting for transfers between devices: 290 us -> none  [the longest x1 65.3 us: body(): lax.all_gather(up_weight, ('seq', 'dp'), axis=0, tiled=True)]
    pallas_call x0 -> x1, Pallas kernels: none -> 260 us  [call_kernel(): pl.pallas_call(make_kernel(seq_size, block, width, ff_half), out_shape=ou...]
    all_gather x4 -> x0, blocking collectives: 140 us -> none  [the longest x2 54.4 us: prefix_2(): lax.all_gather(a.astype(kind), axis)]
    concatenate x2 -> x3, local copies, waits for them, and re-layouts: 118 us -> 0.02 us  [ff_joined(): jnp.concatenate([by[f'{letter}{j}'] for j in range(len(parts))], axis=2)]
    dot_general x35 -> x0, matrix products: 100 us -> none  [the longest x7 28.1 us: matmul(): return jnp.dot(left, right, preferred_element_type=jnp.float32)]
    unnamed x119 -> x52, local copies, waits for them, and re-layouts: 56.5 us -> 10.3 us
    unnamed x1 -> x0, blocking collectives: 41 us -> none
  transfers between devices with their start and end apart: 8 -> 0, of which waited for: 7 -> 0; matrix products, arithmetic and copies ran while one was open for 6% -> 0% of each run, Pallas kernels for 0% -> 0%
where the time goes in v1:
time: 283 us; the launch traced here: 282 us
  Pallas kernels  260 us (92%)
  local copies, waits for them, and re-layouts  14.2 us (5%)
  other arithmetic  7.51 us (3%)
    pallas_call x1, Pallas kernels, call_kernel(): pl.pallas_call(make_kernel(seq_size, block, width, ff_half), out_shape=ou...  260 us
    unnamed x52, local copies, waits for them, and re-layouts  10.3 us

profile of v1, /device:TPU:1, one launch (start us, length us, event | category | flops | bytes accessed | tf_op | source)
XLA Modules:
  0.0 282.4 jit_solution(12705793365638617745)
XLA Ops:
  0.6 0.0 copy-start
  0.7 0.9 pad.15
  1.6 0.0 copy-start.3
  1.7 0.9 copy-done.3
  2.6 0.7 pad_maximum_fusion.3
  3.4 0.7 pad_maximum_fusion.7.refs_7_
  4.0 0.3 copy-done.4
  4.3 0.0 copy-start.19
  4.4 0.7 fusion.1
  5.0 0.0 copy-done
  5.0 0.0 copy-done.19
  5.1 0.8 copy-done.15
  5.9 0.6 pad_maximum_fusion.6.refs_3_
  6.5 0.7 copy-done.20
  7.2 0.0 copy-done.21
  7.2 0.0 copy-start.16
  7.2 0.1 tile.10
  7.3 0.6 pad_maximum_fusion.10.refs_2_
  7.9 0.6 slice.134.refs_10_
  8.6 0.0 copy-done.16
  8.6 0.6 copy.46
  9.2 259.8 %shard_map.194 = (bf16[256,1024]{1,0:T(8,128)(2,1)}, f32[256,1024]{1,0:T(8,128)}, f32[2,32,512]{2,1,0:T(8,128)}, f32[2,32,512]{2,1,0:T(8,128)}, f32[2,32,384]{2,...) custom-call(bf16[256,1024]{1,0:T(8,128)(2,1)} %bitcast.103, ...), custom_call_target="tpu_custom_call" | custom-call | tf_op jit(solution)/shard_map/pallas_call | solution.py:886
  269.0 0.0 copy-start.11
  269.0 0.9 constant_dynamic-update-slice_fusion.8
  269.9 0.0 copy-done.11
  269.9 0.0 copy-start.14
  270.0 0.9 copy-done.14
  270.9 0.0 copy-start.10
  270.9 0.8 fusion
  271.6 0.2 copy-done.10
  271.8 0.9 copy-done.9
  272.7 0.9 copy-done.13
  273.7 0.0 copy-start.8
  273.7 0.8 pad_maximum_fusion.1
  274.4 0.2 copy-done.8
  274.6 0.9 copy-done.7
  275.5 0.9 copy-done.12
  276.4 0.8 pad_maximum_fusion.2
  277.2 0.1 copy-done.17
  277.3 0.0 copy-start.18
  277.3 0.6 pad_maximum_fusion.9
  277.9 0.6 pad_maximum_fusion.8
  278.5 0.0 copy-done.6
  278.5 0.7 maximum_bitcast_fusion
  279.2 0.7 pad_maximum_fusion.5
  279.9 0.7 slice_reduce_fusion
  280.6 0.8 copy.56
  281.4 1.0 copy.57
  (49 shorter events, 0.4 us)
Async XLA Ops:
  0.6 4.4 %copy-start = (bf16[32,256]{1,0:T(8,128)(2,1)S(1)}, bf16[32,256]{1,0:T(8,128)(2,1)}, u32[]{:S(2)}) copy-start(bf16[32,256]{1,0:T(8,128)(2,1)} %param.13) | copy-start | bytes 49156
  1.6 0.9 copy-start.3
  3.3 1.0 copy-start.4
  4.3 0.7 copy-start.19
  5.0 0.8 copy-start.15
  6.5 0.7 copy-start.20
  6.5 0.7 copy-start.21
  7.2 1.4 copy-start.16
  269.0 1.0 copy-start.11
  269.9 0.9 copy-start.14
  270.9 0.9 copy-start.10
  271.8 0.9 copy-start.9
  272.7 0.9 copy-start.13
  273.7 0.9 copy-start.8
  274.6 0.9 copy-start.7
  275.5 0.9 copy-start.12
  276.4 0.8 copy-start.17
  277.3 1.3 copy-start.6
  277.3 1.9 copy-start.5
  277.3 2.6 copy-start.18
  278.5 2.1 copy-start.2
  278.5 2.9 %copy-start.1 = (f32[256,1024]{1,0:T(8,128)S(1)}, f32[256,1024]{1,0:T(8,128)}, u32[]{:S(2)}) copy-start(f32[256,1024]{1,0:T(8,128)} %get-tuple-element.27) | copy-start | bytes 3145732

commit v2 on v1

v2 whole, which is shorter than its diff:
```python
import jax
import jax.numpy as jnp
from jax import lax
from jax.experimental import pallas as pl
from jax.experimental.pallas import tpu as pltpu
from jax.sharding import PartitionSpec as P

HEADS = 16
FDIM = 16
VDIM = 64
EPS = 1e-05
LIN = FDIM**-0.25
QUAD = (2.0 * FDIM) ** -0.5
SHIFTS = FDIM // 2
HALF = FDIM // 2
FEATS = FDIM * (SHIFTS + 2)
HALF_HEADS = HEADS // 2
QH = HALF_HEADS * FDIM
VH = HALF_HEADS * VDIM
PAIRS = HALF_HEADS // 2
COUNTS = PAIRS * FEATS
STATE = COUNTS + 16
STATE_STEPS = STATE // 16
LANES = 128
PIECE = 512
RING = 6
MESH = pl.DeviceIdType.MESH
F32 = jnp.float32
BF16 = jnp.bfloat16


def pieces_of(width):
    out, at = [], 0
    while at < width:
        out.append((at, min(PIECE, width - at)))
        at += PIECE
    return out


def tiles_of(width):
    out, at = [], 0
    while at < width:
        out.append((at, min(256, width - at)))
        at += 256
    return out


def nn(a, b):
    return jnp.dot(a, b, preferred_element_type=F32)


def nt(a, b):
    return lax.dot_general(a, b, (((1,), (1,)), ((), ())), preferred_element_type=F32)


def tn(a, b):
    return lax.dot_general(a, b, (((0,), (0,)), ((), ())), preferred_element_type=F32)


def ahead(t, d):
    return t if d == 0 else pltpu.roll(t, FDIM - d, 0)


def behind(t, d):
    return t if d == 0 else pltpu.roll(t, d, 0)


def features(u):
    rows = [u * ahead(u, d) * QUAD for d in range(SHIFTS)]
    spot = lax.broadcasted_iota(jnp.int32, u.shape, 0)
    last = jnp.where(spot < HALF, u * ahead(u, HALF) * QUAD, jnp.where(spot == HALF, 1.0, 0.0))
    return jnp.concatenate(rows + [last, u * LIN], axis=0).astype(BF16)


def weighted(f):
    at = FDIM * SHIFTS
    scale = jnp.where(lax.broadcasted_iota(jnp.int32, (FDIM, f.shape[1]), 0) < HALF, 2.0, 1.0).astype(BF16)
    return jnp.concatenate([f[:FDIM], f[FDIM:at] * 2, f[at : at + FDIM] * scale, f[at + FDIM :]], axis=0)


def features_back(u, df):
    at = FDIM * SHIFTS
    total = df[at + FDIM :] * LIN
    for d in range(SHIFTS + 1):
        t = df[FDIM * d : FDIM * (d + 1)] * (QUAD * (2.0 if d else 1.0))
        if d == HALF:
            t = jnp.where(lax.broadcasted_iota(jnp.int32, t.shape, 0) < HALF, t, 0.0)
        total = total + t * ahead(u, d) + behind(t * u, d)
    return total


def split_low(u):
    high = u.astype(BF16)
    return high, (u - high.astype(F32)).astype(BF16)


def plan(ff_half):
    parts = pieces_of(ff_half)
    gather = [("gain", LANES), ("qk", 2 * QH), ("v", VH), ("out", VH)]
    for j, (_, w) in enumerate(parts):
        gather += [(f"g{j}", w), (f"u{j}", w)]
    gather += [(f"d{j}", w) for j, (_, w) in enumerate(parts)][1:]
    gather += [("d0", parts[0][1])]
    reduce = [(f"d{j}", w) for j, (_, w) in enumerate(parts)]
    for j, (_, w) in enumerate(parts):
        reduce += [(f"g{j}", w), (f"u{j}", w)]
    reduce += [("out", VH), ("qk", 2 * QH), ("v", VH), ("gain", LANES)]
    return gather, reduce


def offsets_of(chunks):
    out, at = [], 0
    for _, w in chunks:
        out.append(at)
        at += w
    return out


def make_kernel(seq_size, block, width, ff, ff_half):
    gather, reduce = plan(ff_half)
    parts = pieces_of(ff_half)
    n_parts = len(parts)
    gi = {name: i for i, (name, _) in enumerate(gather)}
    ri = {name: i for i, (name, _) in enumerate(reduce)}
    members = seq_size // 8
    n_hi = seq_size // 2
    rows = width // 32
    rows2 = 2 * rows
    quarter = width // 4
    offsets = offsets_of(reduce)
    pack_at = offsets_of(gather)

    def kernel(*refs):
        it = iter(refs)
        take = lambda n: [next(it) for _ in range(n)]
        tok, cot = take(2)
        attn_in, q_in, k_in, v_in, o_in, ffn_in_gain, g_in, u_in, d_in = take(9)
        out_ref, din_ref, go = take(3)
        W = take(len(gather))
        G = take(len(reduce))
        (PK, R1, R2, R3, RZ, RY, FS, X, DY, NB, N1T, N2T, DYT, HID, CA, CB, X1, SND, RCV, OWN) = take(20)
        (NUM, DATT, QK, VT, ATT, DEN, DNUM, DDEN, DQK, DV, DQKV) = take(11)
        (ST, SA, SZ, TZ, TY, SB, PB, PX, WACC, TG, TU, GROW, GACC) = take(13)
        ss, rs, ls = take(3)

        s, dp = lax.axis_index("seq"), lax.axis_index("dp")
        hi, x = s // 2, lax.rem(s, 2)
        y, c = dp // 2, lax.rem(dp, 2)
        g, m = hi // members, lax.rem(hi, members)
        o = 1 - c
        ax, ay = x + o * (1 - 2 * x), y + c * (1 - 2 * y)
        bx, by = x + c * (1 - 2 * x), y + o * (1 - 2 * y)
        p, pa = 2 * x + y, 2 * ax + ay
        pb, pab = 2 * bx + by, 2 * (1 - x) + (1 - y)

        def dev(hi_, x_, y_, c_):
            return (hi_ * 2 + x_, y_ * 2 + c_)

        partner = dev(hi, x, y, o)
        dev_a, dev_b = dev(hi, ax, ay, c), dev(hi, bx, by, c)
        dev_x = dev(hi, 1 - x, y, c)
        ups = [lax.rem(g + j, 4) for j in range(4)]
        downs = [lax.rem(g + 4 - j, 4) for j in range(4)]
        dev_up = [dev(u * members + m, x, y, c) for u in ups]
        right = dev(jnp.minimum(hi + 1, n_hi - 1), x, y, c)
        left = dev(jnp.maximum(hi - 1, 0), x, y, c)

        n_local = [0]
        local_pending = []

        def local(src, dst):
            d = pltpu.make_async_copy(src, dst, ls.at[n_local[0]])
            n_local[0] += 1
            d.start()
            return d

        barrier = pltpu.get_barrier_semaphore()
        greet = [partner, dev_a, dev_b] + dev_up[1:]
        for d in greet:
            pl.semaphore_signal(barrier, inc=1, device_id=d, device_id_type=MESH)
        if members > 1:

            @pl.when(hi < n_hi - 1)
            def _():
                pl.semaphore_signal(barrier, inc=1, device_id=right, device_id_type=MESH)

            @pl.when(hi > 0)
            def _():
                pl.semaphore_signal(barrier, inc=1, device_id=left, device_id_type=MESH)

        cx = local(tok, X.at[c])
        cy = local(cot, DY.at[c])
        cx.wait()
        cy.wait()
        pl.semaphore_wait(barrier, len(greet))
        if members > 1:

            @pl.when(hi < n_hi - 1)
            def _():
                pl.semaphore_wait(barrier, 1)

            @pl.when(hi > 0)
            def _():
                pl.semaphore_wait(barrier, 1)

        numbers = {}
        pending = {}

        def number(key):
            return numbers.setdefault(key, len(numbers))

        def remote(key, src, dst, to):
            i = number(key)
            return pltpu.make_async_remote_copy(
                src_ref=src, dst_ref=dst, send_sem=ss.at[i], recv_sem=rs.at[i], device_id=to, device_id_type=MESH
            )

        def send(key, src, dst, to):
            if key in pending:
                sent(key)
            d = remote(key, src, dst, to)
            d.start()
            pending[key] = d

        def sent(key):
            pending.pop(key).wait_send()

        def got(key, ref):
            remote(key, ref, ref, partner).wait_recv()

        def pack(i, lower, upper):
            w = gather[i][1]
            r = 16 if i == 0 else rows
            mine = W[i].at[g, p, pl.ds(pl.multiple_of(r * c, r), r)]
            stage = PK.at[0:r, pack_at[i] : pack_at[i] + w]

            @pl.when(c == 0)
            def _():
                mine[...] = lower()
                stage[...] = upper()

            @pl.when(c == 1)
            def _():
                mine[...] = upper()
                stage[...] = lower()

            send(("e0", i), stage, mine, partner)

        def ff_piece(ref, at, w):
            have = min(w, ff - at)
            if have == w:
                return ref[:, at : at + w]
            return jnp.concatenate([ref[:, at : at + have], jnp.zeros((ref.shape[0], w - have), BF16)], axis=1)

        def gain_block():
            out = jnp.zeros((16, LANES), F32)
            lanes = lax.broadcasted_iota(jnp.int32, (16, LANES), 1) // rows
            row = lax.broadcasted_iota(jnp.int32, (16, LANES), 0)
            for n, ref in enumerate((attn_in, ffn_in_gain)):
                t = jnp.concatenate([ref[...].astype(F32)] * (LANES // rows), axis=1)
                out = jnp.where((lanes == dp) & (row == n), t, out)
            return out.astype(BF16)

        def e0(i):
            name, w = gather[i]
            if name == "gain":
                pack(i, gain_block, gain_block)
            elif name == "qk":
                pack(
                    i,
                    lambda: jnp.concatenate([q_in[:, :QH], k_in[:, :QH]], axis=1),
                    lambda: jnp.concatenate([q_in[:, QH:], k_in[:, QH:]], axis=1),
                )
            elif name == "v":
                pack(i, lambda: v_in[:, :VH], lambda: v_in[:, VH:])
            elif name == "out":
                pack(i, lambda: o_in[:, :VH], lambda: o_in[:, VH:])
            else:
                at = parts[int(name[1:])][0]
                ref = {"g": g_in, "u": u_in, "d": d_in}[name[0]]
                pack(i, lambda: ff_piece(ref, at, w), lambda: ff_piece(ref, ff_half + at, w))

        def e1(i):
            r = 16 if i == 0 else rows
            got(("e0", i), W[i].at[g, p, pl.ds(pl.multiple_of(r * o, r), r)])
            for j in (1, 2, 3):
                send(("e1", i, j), W[i].at[g, p], W[i].at[g, p], dev_up[j])

        def e2(i):
            for j in (1, 2, 3):
                got(("e1", i, j), W[i].at[downs[j], p])
            send(("e2b", i), W[i].at[:, p], W[i].at[:, p], dev_b)
            send(("e2a", i), W[i].at[:, p], W[i].at[:, p], dev_a)

        def e3(i):
            got(("e2a", i), W[i].at[:, pa])
            send(("e3", i), W[i].at[:, pa], W[i].at[:, pa], dev_b)

        def e4(i):
            got(("e2b", i), W[i].at[:, pb])
            got(("e3", i), W[i].at[:, pab])

        iz = len(gather) - 1

        def z1():
            r = rows
            got(("e0", iz), W[iz].at[g, p, pl.ds(pl.multiple_of(r * o, r), r)])
            send(("e2b", iz), W[iz].at[g, p], W[iz].at[g, p], dev_b)
            send(("e2a", iz), W[iz].at[g, p], W[iz].at[g, p], dev_a)

        def z2():
            got(("e2a", iz), W[iz].at[g, pa])
            send(("e3", iz), W[iz].at[g, pa], W[iz].at[g, pa], dev_b)

        def z3():
            got(("e2b", iz), W[iz].at[g, pb])
            got(("e3", iz), W[iz].at[g, pab])
            for j in (1, 2, 3):
                send(("e1", iz, j), W[iz].at[g], W[iz].at[g], dev_up[j])

        def z4():
            for j in (1, 2, 3):
                got(("e1", iz, j), W[iz].at[downs[j]])

        gathered = {1: -1, 2: -1, 3: -1, 4: -1}

        def ga(step, last):
            while gathered[step] < min(last, iz - 1):
                gathered[step] += 1
                (e1, e2, e3, e4)[step - 1](gathered[step])

        def gstep(k, l1=1, l2=1):
            ga(1, k + l1 + l2)
            ga(2, k + l2)
            ga(3, k)
            ga(4, k - 1)

        done = {1: 0, 2: 0, 3: 0, 4: 0}

        def zf1():
            w = reduce[0][1]
            for j in (1, 2, 3):
                send(("z1", j), G[0].at[ups[j]], RZ.at[j - 1, :, :, 0:w], dev_up[j])

        def zf2():
            w = reduce[0][1]
            for j in (1, 2, 3):
                got(("z1", j), RZ.at[j - 1, :, :, 0:w])

            def one(k):
                total = G[0][g, k].astype(F32)
                for j in range(3):
                    total = total + RZ[j, k, :, 0:w].astype(F32)
                G[0][g, k] = total.astype(BF16)

            loop(4, one)
            for n, q in ((0, pab), (1, pb)):
                send(("z2", n), G[0].at[g, q], RY.at[n, :, 0:w], dev_b)

        def zf3():
            w = reduce[0][1]
            got(("z2", 0), RY.at[0, :, 0:w])
            G[0][g, pa] = G[0][g, pa] + RY[0, :, 0:w]
            send(("z3", 0), G[0].at[g, pa], RY.at[2, :, 0:w], dev_a)
            got(("z2", 1), RY.at[1, :, 0:w])
            G[0][g, p] = G[0][g, p] + RY[1, :, 0:w]

        def zf4():
            w = reduce[0][1]
            got(("z3", 0), RY.at[2, :, 0:w])
            finish_chunk(0, G[0][g, p].astype(F32) + RY[2, :, 0:w].astype(F32))

        def f1(i):
            w = reduce[i][1]
            k = i % RING
            for n, col in ((0, pab), (1, pb)):
                send(("f1", k, n), G[i].at[:, col], R1.at[k, n, :, :, 0:w], dev_b)

        def f2(i):
            w = reduce[i][1]
            k = i % RING
            got(("f1", k, 0), R1.at[k, 0, :, :, 0:w])
            G[i][:, pa] = G[i][:, pa] + R1[k, 0, :, :, 0:w]
            send(("f2", k), G[i].at[:, pa], R2.at[k, :, :, 0:w], dev_a)
            got(("f1", k, 1), R1.at[k, 1, :, :, 0:w])
            G[i][:, p] = G[i][:, p] + R1[k, 1, :, :, 0:w]

        def f3(i):
            w = reduce[i][1]
            k = i % RING
            got(("f2", k), R2.at[k, :, :, 0:w])
            G[i][:, p] = G[i][:, p] + R2[k, :, :, 0:w]
            for j in (1, 2, 3):
                send(("f3", k, j), G[i].at[ups[j], p], R3.at[k, j - 1, :, 0:w], dev_up[j])

        def f4(i):
            w = reduce[i][1]
            k = i % RING
            total = G[i][g, p].astype(F32)
            for j in (1, 2, 3):
                got(("f3", k, j), R3.at[k, j - 1, :, 0:w])
                total = total + R3[k, j - 1, :, 0:w].astype(F32)
            finish_chunk(i, total)

        def finish_chunk(i, total):
            w, at = reduce[i][1], offsets[i]
            FS[:, :, at : at + w] = total.reshape(2, rows, w)
            local_pending.append(local(FS.at[c, :, at : at + w], go.at[c, :, at : at + w]))
            send(("f4", i), FS.at[o, :, at : at + w], go.at[c, :, at : at + w], partner)

        stages = {1: f1, 2: f2, 3: f3, 4: f4}

        def go_to(stage, last):
            while done[stage] < last:
                i = done[stage] + 1
                if stage < 4 and i >= RING // 2:
                    go_to(stage + 1, i - RING // 2)
                if stage > 1:
                    go_to(stage - 1, i)
                stages[stage](i)
                done[stage] = i

        def loop(n, body):
            def step(i, carry):
                body(i)
                return carry

            lax.fori_loop(0, n, step, 0)

        def put_grad(i, lhs_t, rhs):
            w = reduce[i][1]

            def one(k):
                a = lhs_t[pl.ds(pl.multiple_of(k * quarter, quarter), quarter), :]
                G[i][k] = nn(a, rhs()).astype(BF16).reshape(4, rows2, w)

            loop(4, one)

        def weight(i, at, w):
            return W[i][:, :, :, at : at + w].reshape(width, w)

        def transpose_in(src, dst, b):
            def one(k):
                at = pl.multiple_of(k * quarter, quarter)
                dst[pl.ds(at, quarter), pl.ds(pl.multiple_of(b * block, block), block)] = (
                    src[b, :, pl.ds(at, quarter)].astype(F32).T.astype(BF16)
                )

            loop(4, one)

        step_rows = 16
        iq, iv, io = gi["qk"], gi["v"], gi["out"]

        def gains():
            for k in range(8):
                kg, kx = k // 2, k % 2
                acc = None
                for ky in range(2):
                    for kc in range(2):
                        t = W[0][kg, 2 * kx + ky, 16 * kc : 16 * kc + 16, :].astype(F32)
                        acc = t if acc is None else acc + t
                GROW[:, LANES * k : LANES * (k + 1)] = acc[:8]
            GACC[...] = jnp.zeros_like(GACC)

            GACC[...] = jnp.zeros_like(GACC)

        def norm_one(r):
            at = pl.multiple_of(r * step_rows, step_rows)
            for b in range(2):
                xs = X[b, pl.ds(at, step_rows), :].astype(F32)
                r1 = lax.rsqrt(jnp.mean(xs * xs, axis=-1, keepdims=True) + EPS)
                NB[b, pl.ds(at, step_rows), :] = (xs * r1 * GROW[0:1, :]).astype(BF16)

        def first_norm():
            loop(block // step_rows, norm_one)
            transpose_in(NB, N1T, 0)
            transpose_in(NB, N1T, 1)

        def qkv():
            both = NB[...].reshape(2 * block, width)
            t = nn(both, weight(iq, 0, 2 * QH))
            for b in range(2):
                QK[b] = t[block * b : block * (b + 1)].T
            for at, w in tiles_of(VH):
                t = nn(both, weight(iv, at, w))
                for b in range(2):
                    VT[b, at : at + w, :] = t[block * b : block * (b + 1)].T.astype(BF16)

        lane = lax.broadcasted_iota(jnp.int32, (FEATS, LANES), 1)

        def place(i):
            b = i // PAIRS
            hp = lax.rem(i, PAIRS)
            return b, hp

        def slot(hp):
            return pl.ds(pl.multiple_of(FEATS * hp, FEATS), FEATS)

        def q_rows(b, hp, e):
            return QK[b, pl.ds(pl.multiple_of(hp * 2 * FDIM + e * FDIM, FDIM), FDIM), :]

        def k_rows(b, hp, e):
            return QK[b, pl.ds(pl.multiple_of(QH + hp * 2 * FDIM + e * FDIM, FDIM), FDIM), :]

        def v_slice(hp):
            return pl.ds(pl.multiple_of(hp * 2 * VDIM, 2 * VDIM), 2 * VDIM)

        def head_slice(hp, e):
            return pl.ds(pl.multiple_of(hp * 2 * VDIM + e * VDIM, VDIM), VDIM)

        def put_state(i, f0, f1, right_side, w0, w1):
            low = nt(f0, right_side)
            high = nt(f1, right_side)
            b, hp = place(i)
            ST[b, slot(hp), :] = jnp.where(lane < VDIM, low, high).astype(BF16)
            for e, t in ((0, w0), (1, w1)):
                WACC[b, pl.ds(2 * hp + e, 1), :] = t[0:1, :LANES]
                WACC[b, pl.ds(HALF_HEADS + 2 * hp + e, 1), 0 : FEATS - LANES] = t[0:1, LANES:]

        def state_step(i):
            b, hp = place(i)
            fs = [features(k_rows(b, hp, e)) for e in range(2)]
            ws = [nt(jnp.ones((8, block), BF16), f) for f in fs]
            put_state(i, fs[0], fs[1], VT[b, v_slice(hp), :], ws[0], ws[1])

        def states():
            WACC[...] = jnp.zeros_like(WACC)
            loop(2 * PAIRS, state_step)
            ST[:, COUNTS:, :] = WACC[...].astype(BF16)

        ranks = (hi, n_hi - 1 - hi)
        firsts = (x == 0, x == 1)
        doubling = n_hi == 4

        def away(n, j):
            t = hi + j if n == 0 else hi - j
            return dev(jnp.clip(t, 0, n_hi - 1), x, y, c)

        def state_rows(body):
            def step(i, z):
                body(pl.ds(pl.multiple_of(i * 16, 16), 16))
                return z

            lax.fori_loop(0, STATE_STEPS, step, 0)

        def state_x(n):
            send(("sx", n), ST.at[1 - x], SA.at[n], dev_x)

        def near(n):
            return remote(("sz", n, 0), TZ, SZ.at[n, 0], away(n, 1))

        def far(n, j):
            return remote(("sz", n, j), TY, SZ.at[n, 1], away(n, j))

        def near_sends(n):
            return lax.rem(ranks[n], 2) == 0 if doubling else ranks[n] < n_hi - 1

        def near_gets(n):
            return lax.rem(ranks[n], 2) == 1 if doubling else ranks[n] > 0

        def state_z(n):
            got(("sx", n), SA.at[n])
            for j in range(3):
                number(("sz", n, j))

            @pl.when(jnp.logical_not(near_gets(n)))
            def _():
                SZ[n, 0] = jnp.zeros((STATE, LANES), BF16)

            @pl.when(ranks[n] < 2 if doubling else ranks[n] >= 0)
            def _():
                SZ[n, 1] = jnp.zeros((STATE, LANES), BF16)

            if not doubling:

                @pl.when(near_gets(n))
                def _():
                    got(("sz", n, 0), SZ.at[n, 0])

            def add(r):
                t = ST[x, r, :].astype(F32) + SA[n, r, :].astype(F32)
                if not doubling:
                    t = t + SZ[n, 0, r, :].astype(F32)
                TZ[r, :] = t.astype(BF16)

            state_rows(add)
            pl.when(near_sends(n))(lambda: near(n).start())

        def state_far(n):
            if not doubling:
                return

            @pl.when(ranks[n] == 1)
            def _():
                got(("sz", n, 0), SZ.at[n, 0])

                def add(r):
                    TY[r, :] = (TZ[r, :].astype(F32) + SZ[n, 0, r, :].astype(F32)).astype(BF16)

                state_rows(add)
                far(n, 1).start()
                far(n, 2).start()

        def state_end(n, dst):
            if doubling:

                @pl.when(ranks[n] == 3)
                def _():
                    got(("sz", n, 0), SZ.at[n, 0])
                    got(("sz", n, 2), SZ.at[n, 1])

                @pl.when(ranks[n] == 2)
                def _():
                    got(("sz", n, 1), SZ.at[n, 1])

            def add(r):
                total = SZ[n, 0, r, :].astype(F32) + SZ[n, 1, r, :].astype(F32)
                mine = ST[x, r, :].astype(F32)
                other = SA[n, r, :].astype(F32)
                dst[x, r, :] = (total + jnp.where(firsts[n], 0.0, other)).astype(BF16)
                SB[r, :] = (total + jnp.where(firsts[n], mine, 0.0)).astype(BF16)

            state_rows(add)
            send(("sy", n), SB, dst.at[x], dev_x)

        def state_got(n, dst):
            got(("sy", n), dst.at[1 - x])

        def state_sent(n):
            sent(("sx", n))
            sent(("sy", n))
            pl.when(near_sends(n))(lambda: near(n).wait_send())
            if doubling:

                @pl.when(ranks[n] == 1)
                def _():
                    far(n, 1).wait_send()
                    far(n, 2).wait_send()

        def score_z(b, hp, e):
            qh, ql = split_low(q_rows(b, hp, e))
            kh, kl = split_low(k_rows(b, hp, e))
            return tn(jnp.concatenate([kh, kh, kl], axis=0), jnp.concatenate([qh, ql, qh], axis=0))

        def counts(buf, b):
            return buf[b, COUNTS:, :]

        def count_dot(t, f, at):
            r = nn(t[:HALF_HEADS], f[:LANES]) + nn(t[HALF_HEADS:, : FEATS - LANES], f[LANES:])
            spot = lax.broadcasted_iota(jnp.int32, r.shape, 0)
            return jnp.sum(jnp.where(spot == at, r, 0.0), axis=0, keepdims=True)

        def count_outer(t, row, at):
            spot = lax.broadcasted_iota(jnp.int32, (16, block), 0)
            first = jnp.where(spot == at, row, 0.0).astype(BF16)
            second = jnp.where(spot == HALF_HEADS + at, row, 0.0).astype(BF16)
            return jnp.concatenate([tn(t, first), tn(t[:, : FEATS - LANES], second)], axis=0)

        def att_step(i):
            b, hp = place(i)
            turned = PB[b, slot(hp), :].astype(F32).T.astype(BF16)
            tops = []
            for e in range(2):
                z = score_z(b, hp, e)
                st = (1.0 + z * FDIM**-0.5 + z * z * (0.5 / FDIM)).astype(BF16)
                fq = weighted(features(q_rows(b, hp, e)))
                num = nn(VT[b, head_slice(hp, e), :], st) + nn(turned[VDIM * e : VDIM * (e + 1)], fq)
                den = jnp.sum(st.astype(F32), axis=0, keepdims=True) + count_dot(counts(PB, b), fq, 2 * hp + e)
                NUM[b, head_slice(hp, e), :] = num
                DEN[i, e : e + 1, :] = den
                tops.append(num / den)
            ATT[b, :, v_slice(hp)] = jnp.concatenate(tops, axis=0).T.astype(BF16)

        def attention():
            loop(2 * PAIRS, att_step)

        def col(k):
            return pl.ds(pl.multiple_of(k * quarter, quarter), quarter)

        def wrow(i, k, at, w):
            return W[i][k, :, :, at : at + w].reshape(quarter, w)

        def out_proj(dst, b):
            def one(k):
                dst[:, col(k)] = nt(ATT[b], wrow(io, k, 0, VH))

            loop(4, one)

        def proj_send():
            out_proj(SND.at[0], o)
            send("x1", SND.at[0], RCV.at[0], partner)

        def norm_two(r):
            at = pl.multiple_of(r * step_rows, step_rows)
            rr = pl.ds(at, step_rows)
            x1 = X[c, rr, :].astype(F32) + (OWN[rr, :] + RCV[0, rr, :])
            X1[rr, :] = x1
            r2 = lax.rsqrt(jnp.mean(x1 * x1, axis=-1, keepdims=True) + EPS)
            NB[c, rr, :] = (x1 * r2 * GROW[1:2, :]).astype(BF16)

        def second_norm():
            out_proj(OWN, c)
            got("x1", RCV.at[0])
            loop(block // step_rows, norm_two)
            send("n2", NB.at[c], NB.at[c], partner)
            transpose_in(NB, N2T, c)
            got("n2", NB.at[o])
            transpose_in(NB, N2T, o)

        def ffn_in(j):
            base, w = parts[j]
            for at, tw in tiles_of(w):
                TG[:, 0:tw] = nn(NB[...].reshape(2 * block, width), weight(gi[f"g{j}"], at, tw))
                TU[:, 0:tw] = nn(NB[...].reshape(2 * block, width), weight(gi[f"u{j}"], at, tw))
                lo = base + at

                def one(r):
                    rr = pl.ds(pl.multiple_of(r * 64, 64), 64)
                    gate, up = TG[rr, 0:tw], TU[rr, 0:tw]
                    sg = 1.0 / (1.0 + jnp.exp(-gate))
                    silu = gate * sg
                    HID[rr, lo : lo + tw] = (silu * up).astype(BF16)
                    CA[rr, lo : lo + tw] = (up * sg * (1.0 + gate * (1.0 - sg))).astype(BF16)
                    CB[rr, lo : lo + tw] = silu.astype(BF16)

                loop(2 * block // 64, one)
        def ffn_back(j):
            base, w = parts[j]
            i = gi[f"d{j}"]
            for at, tw in tiles_of(w):
                TG[:, 0:tw] = nn(DY[...].reshape(2 * block, width), weight(i, at, tw))
                lo = base + at

                def one(r):
                    rr = pl.ds(pl.multiple_of(r * 64, 64), 64)
                    dh = TG[rr, 0:tw]
                    CA[rr, lo : lo + tw] = (dh * CA[rr, lo : lo + tw].astype(F32)).astype(BF16)
                    CB[rr, lo : lo + tw] = (dh * CB[rr, lo : lo + tw].astype(F32)).astype(BF16)

                loop(2 * block // 64, one)

        def tokens_of(b):
            return pl.ds(pl.multiple_of(b * block, block), block)

        def dn2(dst, b):
            def one(k):
                acc = None
                for j, (base, w) in enumerate(parts):
                    for buf, i in ((CA, gi[f"g{j}"]), (CB, gi[f"u{j}"])):
                        t = nt(buf[tokens_of(b), base : base + w], wrow(i, k, 0, w))
                        acc = t if acc is None else acc + t
                dst[:, col(k)] = acc

            loop(4, one)

        def dn2_send():
            sent("x1")
            dn2(SND.at[0], o)
            send("dn2", SND.at[0], RCV.at[1], partner)
            dn2(OWN, c)

        def norm_two_back(r):
            at = pl.multiple_of(r * step_rows, step_rows)
            rr = pl.ds(at, step_rows)
            d = OWN[rr, :] + RCV[1, rr, :]
            x1 = X1[rr, :]
            r2 = lax.rsqrt(jnp.mean(x1 * x1, axis=-1, keepdims=True) + EPS)
            t = d * (x1 * r2)
            GACC[8:16, :] += t[:8] + t[8:]
            a2 = d * GROW[1:2, :]
            dx = DY[c, rr, :].astype(F32) + (
                r2 * a2 - x1 * (r2 * r2 * r2) * jnp.mean(a2 * x1, axis=-1, keepdims=True)
            )
            din_ref[rr, :] = dx
            NB[c, rr, :] = dx.astype(BF16)

        def second_norm_back():
            got("dn2", RCV.at[1])
            sent("n2")
            loop(block // step_rows, norm_two_back)
            send("dx1", NB.at[c], NB.at[c], partner)
            transpose_in(NB, DYT, c)

        def datt():
            got("dx1", NB.at[o])
            transpose_in(NB, DYT, o)
            for at, tw in tiles_of(VH):
                t = nn(NB[...].reshape(2 * block, width), weight(io, at, tw))
                for b in range(2):
                    DATT[b, at : at + tw, :] = t[block * b : block * (b + 1)].T

        def back_state_step(i):
            b, hp = place(i)
            fs, ws = [], []
            for e in range(2):
                hs = head_slice(hp, e)
                datt, num, den = DATT[b, hs, :], NUM[b, hs, :], DEN[i, e : e + 1, :]
                dd = (-jnp.sum(datt * num, axis=0, keepdims=True) / (den * den)).astype(BF16)
                DNUM[b, hs, :] = (datt / den).astype(BF16)
                DDEN[i, e : e + 1, :] = dd.astype(F32)
                f = features(q_rows(b, hp, e))
                fs.append(f)
                ws.append(nt(jnp.broadcast_to(dd, (8, block)), f))
            put_state(i, fs[0], fs[1], DNUM[b, v_slice(hp), :], ws[0], ws[1])

        def back_states():
            WACC[...] = jnp.zeros_like(WACC)
            state_sent(0)
            loop(2 * PAIRS, back_state_step)
            ST[:, COUNTS:, :] = WACC[...].astype(BF16)

        zeros_head = jnp.zeros((VDIM, block), BF16)

        def masked(t, e):
            return jnp.concatenate([zeros_head, t] if e else [t, zeros_head], axis=0)

        def back_step(i):
            b, hp = place(i)
            for e in range(2):
                hs = head_slice(hp, e)
                q, kk = q_rows(b, hp, e), k_rows(b, hp, e)
                qh, ql = split_low(q)
                kh, kl = split_low(kk)
                z = tn(jnp.concatenate([kh, kh, kl], axis=0), jnp.concatenate([qh, ql, qh], axis=0))
                st = (1.0 + z * FDIM**-0.5 + z * z * (0.5 / FDIM)).astype(BF16)
                dnum, dden = DNUM[b, hs, :], DDEN[i, e : e + 1, :]
                ds = (tn(VT[b, hs, :], dnum) + dden).astype(BF16).astype(F32)
                dz = (ds * (FDIM**-0.5 + z * (1.0 / FDIM))).astype(BF16)
                t = nn(jnp.concatenate([kh, kl], axis=0), dz)
                dq = t[:FDIM] + t[FDIM:]
                t = nt(jnp.concatenate([qh, ql], axis=0), dz)
                dk = t[:FDIM] + t[FDIM:]
                DV[b, hs, :] = nt(dnum, st)
                df = nn(PB[b, slot(hp), :], masked(dnum, e)) + count_outer(counts(PB, b), dden, 2 * hp + e)
                DQK[b, pl.ds(pl.multiple_of(hp * 2 * FDIM + e * FDIM, FDIM), FDIM), :] = dq + features_back(q, df)
                DQK[b, pl.ds(pl.multiple_of(QH + hp * 2 * FDIM + e * FDIM, FDIM), FDIM), :] = dk

        def back_rows(lo, n):
            def step(i, z):
                back_step(lo + i)
                return z

            lax.fori_loop(0, n, step, 0)

        def y_part(dst, b):
            def one(k):
                acc = None
                for j, (base, w) in enumerate(parts):
                    t = nt(HID[tokens_of(b), base : base + w], wrow(gi[f"d{j}"], k, 0, w))
                    acc = t if acc is None else acc + t
                dst[:, col(k)] = acc

            loop(4, one)

        def finish(r):
            rr = pl.ds(pl.multiple_of(r * step_rows, step_rows), step_rows)
            out_ref[rr, :] = (X1[rr, :] + (OWN[rr, :] + RCV[2, rr, :])).astype(BF16)

        def y_send():
            y_part(SND.at[1], o)
            send("y", SND.at[1], RCV.at[2], partner)
            y_part(OWN, c)

        def y_end():
            got("y", RCV.at[2])
            loop(block // step_rows, finish)

        def key_step(i):
            b, hp = place(i)
            turned = PX[b, slot(hp), :].astype(F32).T.astype(BF16)
            for e in range(2):
                hs = head_slice(hp, e)
                kk = k_rows(b, hp, e)
                df = nn(PX[b, slot(hp), :], masked(VT[b, hs, :], e)) + count_outer(
                    counts(PX, b), jnp.ones((1, block), F32), 2 * hp + e
                )
                kr = pl.ds(pl.multiple_of(QH + hp * 2 * FDIM + e * FDIM, FDIM), FDIM)
                DQK[b, kr, :] += features_back(kk, df)
                DV[b, hs, :] += nn(turned[VDIM * e : VDIM * (e + 1)], weighted(features(kk)))

        def keys_back():
            loop(2 * PAIRS, key_step)
            for b in range(2):
                DQKV[b, :, 0 : 2 * QH] = DQK[b].T.astype(BF16)
                for at, tw in tiles_of(VH):
                    DQKV[b, :, 2 * QH + at : 2 * QH + at + tw] = DV[b, at : at + tw, :].T.astype(BF16)

        def dn1(dst, b):
            def one(k):
                dst[:, col(k)] = nt(DQKV[b, :, : 2 * QH], wrow(iq, k, 0, 2 * QH)) + nt(
                    DQKV[b, :, 2 * QH :], wrow(iv, k, 0, VH)
                )

            loop(4, one)

        def dn1_send():
            sent("dn2")
            dn1(SND.at[0], o)
            send("dn1", SND.at[0], RCV.at[0], partner)
            dn1(OWN, c)

        def norm_one_back(r):
            rr = pl.ds(pl.multiple_of(r * step_rows, step_rows), step_rows)
            d = OWN[rr, :] + RCV[0, rr, :]
            xs = X[c, rr, :].astype(F32)
            r1 = lax.rsqrt(jnp.mean(xs * xs, axis=-1, keepdims=True) + EPS)
            t = d * (xs * r1)
            GACC[0:8, :] += t[:8] + t[8:]
            a1 = d * GROW[0:1, :]
            din_ref[rr, :] += r1 * a1 - xs * (r1 * r1 * r1) * jnp.mean(a1 * xs, axis=-1, keepdims=True)

        def first_norm_back():
            got("dn1", RCV.at[0])
            loop(block // step_rows, norm_one_back)
            sum_a = jnp.sum(GACC[0:8, :], axis=0, keepdims=True)
            gf = jnp.sum(GACC[8:16, :], axis=0, keepdims=True)
            last = ri["gain"]
            for k in range(4):
                row = lax.broadcasted_iota(jnp.int32, (LANES, quarter), 0)
                sl = slice(quarter * k, quarter * (k + 1))
                mat = jnp.where(row == 0, sum_a[:, sl], 0.0) + jnp.where(row == 1, gf[:, sl], 0.0)
                G[last][k] = mat.T.astype(BF16).reshape(4, rows2, LANES)
        def part_of(buf, j):
            base, w = parts[j]
            return lambda: buf[:, base : base + w]

        def grad(name):
            kind = name.rstrip("0123456789")
            if kind == "d":
                put_grad(ri[name], DYT, part_of(HID, int(name[1:])))
            elif kind == "g":
                put_grad(ri[name], N2T, part_of(CA, int(name[1:])))
            elif kind == "u":
                put_grad(ri[name], N2T, part_of(CB, int(name[1:])))
            elif name == "out":
                put_grad(ri[name], DYT, lambda: ATT[...].reshape(2 * block, VH))
            elif name == "qk":
                put_grad(ri[name], N1T, lambda: DQKV[:, :, 0 : 2 * QH].reshape(2 * block, 2 * QH))
            elif name == "v":
                put_grad(ri[name], N1T, lambda: DQKV[:, :, 2 * QH :].reshape(2 * block, VH))

        def adv(st, name):
            go_to(st, ri[name])

        for i in range(len(gather)):
            e0(i)
        send("x", X.at[c], X.at[c], partner)
        send("dy", DY.at[c], DY.at[c], partner)
        ga(1, 0)
        gstep(-1)
        gstep(0)
        transpose_in(DY, DYT, c)
        got("x", X.at[o])
        got("dy", DY.at[o])
        transpose_in(DY, DYT, o)
        gstep(1, 2, 1)
        z1()
        gains()
        first_norm()
        gstep(2, 2, 1)
        ga(2, 4)
        ga(4, 2)
        qkv()
        states()
        state_x(0)
        gstep(3, 2, 1)
        z2()
        gstep(4, 2, 1)
        state_z(0)
        gstep(5, 4, 1)
        state_far(0)
        z3()
        gstep(6, 5, 1)
        state_end(0, PB)
        gstep(7, 5, 1)
        state_got(0, PB)
        gstep(8, 5, 2)
        attention()
        gstep(9, 5, 2)
        proj_send()
        second_norm()
        gstep(10, 5, 2)
        ffn_in(0)
        grad("d0")
        zf1()
        ffn_in(1)
        grad("d1")
        adv(1, "d1")
        ga(3, 11)
        ga(4, 9)
        ffn_in(2)
        grad("d2")
        adv(1, "d2")
        z4()
        ffn_back(0)
        adv(2, "d1")
        grad("g0")
        adv(1, "g0")
        ga(4, 10)
        ffn_back(1)
        adv(2, "d2")
        adv(3, "d1")
        ga(4, 11)
        ffn_back(2)
        dn2_send()
        grad("u0")
        adv(1, "u0")
        second_norm_back()
        adv(4, "d1")
        datt()
        back_states()
        state_x(1)
        grad("g1")
        adv(2, "g0")
        adv(3, "d2")
        adv(1, "g1")
        state_z(1)
        zf2()
        adv(4, "d2")
        grad("u1")
        adv(2, "u0")
        adv(3, "g0")
        adv(1, "u1")
        back_rows(0, 4)
        state_far(1)
        grad("g2")
        adv(2, "g1")
        adv(3, "u0")
        adv(4, "g0")
        adv(1, "g2")
        zf3()
        state_end(1, PX)
        back_rows(4, 4)
        grad("u2")
        adv(2, "u1")
        adv(3, "g1")
        adv(4, "u0")
        adv(1, "u2")
        zf4()
        y_send()
        grad("out")
        state_got(1, PX)
        keys_back()
        grad("qk")
        adv(2, "g2")
        adv(3, "u1")
        adv(4, "g1")
        adv(1, "out")
        y_end()
        adv(2, "u2")
        adv(3, "g2")
        adv(4, "u1")
        adv(1, "qk")
        grad("v")
        adv(1, "v")
        dn1_send()
        adv(2, "out")
        adv(3, "u2")
        adv(4, "g2")
        first_norm_back()
        adv(1, "gain")
        adv(2, "qk")
        adv(3, "out")
        adv(4, "u2")
        adv(2, "v")
        adv(3, "qk")

        n = len(reduce)
        for k in range(n, n + 4):
            for st in (1, 2, 3, 4):
                go_to(st, min(n - 1, k - st))
        for i in range(n):
            got(("f4", i), go.at[o, :, offsets[i] : offsets[i] + reduce[i][1]])
        for d in local_pending:
            d.wait()
        state_sent(1)
        for d in pending.values():
            d.wait_send()

    return kernel


def call_kernel(tok, cot, shards, seq_size, ff, ff_half):
    block, width = tok.shape
    gather, reduce = plan(ff_half)
    rows = width // 32
    vmem = pltpu.VMEM
    any_spec = pl.BlockSpec(memory_space=pl.ANY)
    vmem_spec = pl.BlockSpec(memory_space=vmem)
    total_width = sum(w for _, w in reduce)
    pack_width = sum(w for _, w in gather)
    state = vmem((2, STATE, LANES), BF16)
    scratch = [vmem((4, 4, 2 * (16 if name == "gain" else rows), w), BF16) for name, w in gather]
    scratch += [vmem((4, 4, 2 * rows, w), BF16) for _, w in reduce]
    scratch += [
        vmem((rows, pack_width), BF16),
        vmem((RING, 2, 4, 2 * rows, PIECE), BF16),
        vmem((RING, 4, 2 * rows, PIECE), BF16),
        vmem((RING, 3, 2 * rows, PIECE), BF16),
        vmem((3, 4, 2 * rows, PIECE), BF16),
        vmem((3, 2 * rows, PIECE), BF16),
        vmem((2, rows, total_width), F32),
        vmem((2, block, width), BF16),
        vmem((2, block, width), BF16),
        vmem((2, block, width), BF16),
        vmem((width, 2 * block), BF16),
        vmem((width, 2 * block), BF16),
        vmem((width, 2 * block), BF16),
        vmem((2 * block, ff_half), BF16),
        vmem((2 * block, ff_half), BF16),
        vmem((2 * block, ff_half), BF16),
        vmem((block, width), F32),
        vmem((2, block, width), F32),
        vmem((3, block, width), F32),
        vmem((block, width), F32),
        vmem((2, VH, block), F32),
        vmem((2, VH, block), F32),
        vmem((2, 2 * QH, block), F32),
        vmem((2, VH, block), BF16),
        vmem((2, block, VH), BF16),
        vmem((2 * PAIRS, 8, block), F32),
        vmem((2, VH, block), BF16),
        vmem((2 * PAIRS, 8, block), F32),
        vmem((2, 2 * QH, block), F32),
        vmem((2, VH, block), F32),
        vmem((2, block, 2 * QH + VH), BF16),
        state,
        vmem((2, STATE, LANES), BF16),
        vmem((2, 2, STATE, LANES), BF16),
        vmem((STATE, LANES), BF16),
        vmem((STATE, LANES), BF16),
        vmem((STATE, LANES), BF16),
        state,
        state,
        vmem((2, 16, LANES), F32),
        vmem((2 * block, 256), F32),
        vmem((2 * block, 256), F32),
        vmem((8, width), F32),
        vmem((16, width), F32),
        pltpu.SemaphoreType.DMA((n_messages(gather, reduce),)),
        pltpu.SemaphoreType.DMA((n_messages(gather, reduce),)),
        pltpu.SemaphoreType.DMA((2 + len(reduce),)),
    ]
    out_shape = [
        jax.ShapeDtypeStruct((block, width), BF16),
        jax.ShapeDtypeStruct((block, width), F32),
        jax.ShapeDtypeStruct((2, rows, total_width), F32),
    ]
    return pl.pallas_call(
        make_kernel(seq_size, block, width, ff, ff_half),
        out_shape=out_shape,
        in_specs=[any_spec] * 2 + [vmem_spec] * len(shards),
        out_specs=[vmem_spec] * 2 + [any_spec],
        scratch_shapes=scratch,
        compiler_params=pltpu.CompilerParams(
            collective_id=0, has_side_effects=True, vmem_limit_bytes=62 * 2**20
        ),
    )(tok, cot, *shards)


def n_messages(gather, reduce):
    return 7 * len(gather) + 6 * RING + len(reduce) + 24


def call_finish(output, input_grad, grads, ff, ff_half):
    block, width = output.shape
    rows = grads.shape[1]
    _, reduce = plan(ff_half)
    at = dict(zip([name for name, _ in reduce], offsets_of(reduce)))
    parts = pieces_of(ff_half)
    vmem_spec = pl.BlockSpec(memory_space=pltpu.VMEM)
    hbm_spec = pl.BlockSpec(memory_space=pltpu.HBM)

    def kernel(o_in, i_in, g_hbm, o_out, i_out, ag, qg, kg, vg, og, fg, gg, ug, dg, g_in, sems):
        c2 = pltpu.make_async_copy(g_hbm, g_in, sems.at[2])
        c2.start()
        c0 = pltpu.make_async_copy(o_in, o_out, sems.at[0])
        c1 = pltpu.make_async_copy(i_in, i_out, sems.at[1])
        c0.start()
        c1.start()
        c2.wait()
        gain = (g_in[0, :, at["gain"] : at["gain"] + LANES] + g_in[1, :, at["gain"] : at["gain"] + LANES]).T
        ag[...] = gain[0:1, :rows]
        fg[...] = gain[1:2, :rows]
        for h in range(2):
            qg[:, QH * h : QH * (h + 1)] = g_in[h, :, at["qk"] : at["qk"] + QH]
            kg[:, QH * h : QH * (h + 1)] = g_in[h, :, at["qk"] + QH : at["qk"] + 2 * QH]
            vg[:, VH * h : VH * (h + 1)] = g_in[h, :, at["v"] : at["v"] + VH]
            og[:, VH * h : VH * (h + 1)] = g_in[h, :, at["out"] : at["out"] + VH]
            for j, (base, w) in enumerate(parts):
                lo = ff_half * h + base
                have = min(w, ff - lo)
                for ref, letter in ((gg, "g"), (ug, "u"), (dg, "d")):
                    a = at[f"{letter}{j}"]
                    ref[:, lo : lo + have] = g_in[h, :, a : a + have]
        c0.wait()
        c1.wait()

    shapes = [(1, rows), (rows, 2 * QH), (rows, 2 * QH), (rows, 2 * VH), (rows, 2 * VH), (1, rows)] + [(rows, ff)] * 3
    return pl.pallas_call(
        kernel,
        out_shape=[jax.ShapeDtypeStruct(output.shape, BF16), jax.ShapeDtypeStruct(input_grad.shape, F32)]
        + [jax.ShapeDtypeStruct(n, F32) for n in shapes],
        in_specs=[hbm_spec] * 3,
        out_specs=[hbm_spec] * 2 + [vmem_spec] * len(shapes),
        scratch_shapes=[pltpu.VMEM(grads.shape, F32), pltpu.SemaphoreType.DMA((3,))],
        compiler_params=pltpu.CompilerParams(vmem_limit_bytes=32 * 2**20),
    )(output, input_grad, grads)


def body(
    tokens, attn_gain, query_weight, key_weight, value_weight, out_weight, ffn_gain, gate_weight, up_weight, down_weight, cotangent
):
    seq_size = lax.axis_size("seq")
    members = seq_size // 8
    _, block, width = tokens.shape
    ff = gate_weight.shape[1]
    ff_half = LANES * ((ff + 2 * LANES - 1) // (2 * LANES))
    few = attn_gain.shape[0]
    groups = [[(g * members + m) * 2 + x for m in range(members)] for g in range(4) for x in range(2)]

    shards = [attn_gain, query_weight, key_weight, value_weight, out_weight.T, ffn_gain, gate_weight, up_weight, down_weight.T]
    if members > 1:
        shards = [
            lax.all_gather(a, "seq", axis_index_groups=groups, axis=0, tiled=True) for a in shards
        ]
    shards = [a.reshape(1, -1) if a.ndim == 1 else a for a in shards]

    def turn(t):
        if members == 1:
            return t
        return t.reshape(block, 4, members, 2, 4, few).transpose(0, 1, 3, 4, 2, 5).reshape(block, width)

    def turn_back(t):
        if members == 1:
            return t
        return t.reshape(block, 4, 2, 4, members, few).transpose(0, 1, 4, 2, 3, 5).reshape(block, width)

    output, input_grad, grads = call_kernel(turn(tokens[0]), turn(cotangent[0]), shards, seq_size, ff, ff_half)
    if members == 1:
        o, i, ag, qg, kg, vg, og, fg, gg, ug, dg = call_finish(output, input_grad, grads, ff, ff_half)
        return o[None], i[None], ag[0], qg, kg, vg, og.T, fg[0], gg, ug, dg.T
    grads = lax.psum_scatter(grads, "seq", scatter_dimension=1, axis_index_groups=groups, tiled=True)
    _, reduce = plan(ff_half)
    by = {name: grads[:, :, a : a + w] for (name, w), a in zip(reduce, offsets_of(reduce))}
    n_parts = len(pieces_of(ff_half))

    def joined(a):
        return jnp.concatenate([a[0], a[1]], axis=1)

    def ff_joined(letter):
        return joined(jnp.concatenate([by[f"{letter}{j}"] for j in range(n_parts)], axis=2))[:, :ff]

    gain = by["gain"][0] + by["gain"][1]
    return (
        turn_back(output)[None],
        turn_back(input_grad)[None],
        gain[:, 0],
        joined(by["qk"][:, :, :QH]),
        joined(by["qk"][:, :, QH:]),
        joined(by["v"]),
        joined(by["out"]).T,
        gain[:, 1],
        ff_joined("g"),
        ff_joined("u"),
        ff_joined("d").T,
    )


def solution(mesh):
    both = ("seq", "dp")
    row, column, whole = P(both, None), P(None, both), P("dp", "seq", None)
    return jax.shard_map(
        body,
        mesh=mesh,
        in_specs=(whole, P(both), row, row, row, column, P(both), row, row, column, whole),
        out_specs=(whole, whole, P(both), row, row, row, column, P(both), row, row, column),
        check_vma=False,
    )
```

time: 283 us -> 244 us (0.86)
  Pallas kernels: 260 us -> 239 us
  local copies, waits for them, and re-layouts: 14.2 us -> 3.62 us
  other arithmetic: 7.51 us -> 0 us
    pallas_call x1 -> x2, Pallas kernels: 260 us -> 239 us  [the longest x1 236 us: call_kernel(): pl.pallas_call(make_kernel(seq_size, block, width, ff, ff_half), out_shap...]
    unnamed x52 -> x6, local copies, waits for them, and re-layouts: 10.3 us -> 3.62 us
    concatenate x8 -> x0, other arithmetic: 5.45 us -> none  [the longest x5 3.42 us: joined(): return jnp.concatenate([a[0], a[1]], axis=1)]
where the time goes in v2:
time: 244 us; the launch traced here: 243 us
  Pallas kernels  239 us (98%)
  local copies, waits for them, and re-layouts  3.62 us (1%)
    pallas_call x1, Pallas kernels, call_kernel(): pl.pallas_call(make_kernel(seq_size, block, width, ff, ff_half), out_shap...  236 us

profile of v2, /device:TPU:1, one launch (start us, length us, event | category | flops | bytes accessed | tf_op | source)
XLA Modules:
  0.0 243.3 jit_solution(9706064002647676626)
XLA Ops:
  0.6 236.4 %shard_map.194 = (bf16[256,1024]{1,0:T(8,128)(2,1)}, f32[256,1024]{1,0:T(8,128)}, f32[2,32,5632]{2,1,0:T(8,128)}) custom-call(bf16[256,1024]{1,0:T(8,128)(2,1)} %bitcast.12, bf16[256,1024]{1,0:T(8,128)(2,1)} %bitcast.13, bf16[1,32]{1,0:T(2,128)(2,1)} %bitcast.16, bf16[32,256]{1,0:T(8,128)(2,1)} %refs_3_.1, bf16[32,256]{1,0:T(8,128)(2,1)} %refs_4_.1, ...), custom_call_target="tpu_custom_call" | custom-call | tf_op jit(solution)/shard_map/pallas_call | solution.py:1149
  237.0 0.0 copy-start
  237.0 1.4 copy-done
  238.4 0.0 copy-start.1
  238.4 1.2 copy-done.1
  239.6 0.0 copy-start.2
  239.6 1.0 copy-done.2
  240.6 2.5 %shard_map.195 = (bf16[256,1024]{1,0:T(8,128)(2,1)}, f32[256,1024]{1,0:T(8,128)}, f32[1,32]{1,0:T(1,128)}, f32[32,256]{1,0:T(8,128)}, f32[32,256]{1,0:T(8,128)},...) custom-call(bf16[256,1024]{1,0:T(8,128)(2,1)S(1)} %copy-done.2, ...), custom_call_target="tpu_custom_call" | custom-call | tf_op jit(solution)/shard_map/pallas_call | solution.py:1200
Async XLA Ops:
  237.0 1.4 copy-start
  238.4 1.2 copy-start.1
  239.6 1.0 copy-start.2

commit v3 on v2

--- a/solution.py
+++ b/solution.py
@@ -21,7 +21,9 @@
 COUNTS = PAIRS * FEATS
 STATE = COUNTS + 16
 STATE_STEPS = STATE // 16
+SPLIT = 96
 LANES = 128
+ALIKE = (("g0",), ())
 PIECE = 512
 RING = 6
 MESH = pl.DeviceIdType.MESH
@@ -148,17 +150,24 @@
         y, c = dp // 2, lax.rem(dp, 2)
         g, m = hi // members, lax.rem(hi, members)
         o = 1 - c
-        ax, ay = x + o * (1 - 2 * x), y + c * (1 - 2 * y)
-        bx, by = x + c * (1 - 2 * x), y + o * (1 - 2 * y)
-        p, pa = 2 * x + y, 2 * ax + ay
-        pb, pab = 2 * bx + by, 2 * (1 - x) + (1 - y)
+        p, pab = 2 * x + y, 2 * (1 - x) + (1 - y)
 
         def dev(hi_, x_, y_, c_):
             return (hi_ * 2 + x_, y_ * 2 + c_)
 
         partner = dev(hi, x, y, o)
-        dev_a, dev_b = dev(hi, ax, ay, c), dev(hi, bx, by, c)
-        dev_x = dev(hi, 1 - x, y, c)
+        dev_x, dev_y = dev(hi, 1 - x, y, c), dev(hi, x, 1 - y, c)
+
+        def roles(flip):
+            nx, ny = x + flip * (1 - 2 * x), y + (1 - flip) * (1 - 2 * y)
+            return dev(hi, nx, ny, c), 2 * nx + ny
+
+        mixed = roles(o) + roles(c)
+        alike = roles(1) + roles(0)
+
+        def way(name, phase):
+            return alike if name in ALIKE[phase] else mixed
+
         ups = [lax.rem(g + j, 4) for j in range(4)]
         downs = [lax.rem(g + 4 - j, 4) for j in range(4)]
         dev_up = [dev(u * members + m, x, y, c) for u in ups]
@@ -175,7 +184,7 @@
             return d
 
         barrier = pltpu.get_barrier_semaphore()
-        greet = [partner, dev_a, dev_b] + dev_up[1:]
+        greet = [partner, dev_x, dev_y] + dev_up[1:]
         for d in greet:
             pl.semaphore_signal(barrier, inc=1, device_id=d, device_id_type=MESH)
         if members > 1:
@@ -187,21 +196,6 @@
             @pl.when(hi > 0)
             def _():
                 pl.semaphore_signal(barrier, inc=1, device_id=left, device_id_type=MESH)
-
-        cx = local(tok, X.at[c])
-        cy = local(cot, DY.at[c])
-        cx.wait()
-        cy.wait()
-        pl.semaphore_wait(barrier, len(greet))
-        if members > 1:
-
-            @pl.when(hi < n_hi - 1)
-            def _():
-                pl.semaphore_wait(barrier, 1)
-
-            @pl.when(hi > 0)
-            def _():
-                pl.semaphore_wait(barrier, 1)
 
         numbers = {}
         pending = {}
@@ -244,7 +238,11 @@
                 mine[...] = upper()
                 stage[...] = lower()
 
-            send(("e0", i), stage, mine, partner)
+        def e0_send(i):
+            w = gather[i][1]
+            r = 16 if i == 0 else rows
+            mine = W[i].at[g, p, pl.ds(pl.multiple_of(r * c, r), r)]
+            send(("e0", i), PK.at[0:r, pack_at[i] : pack_at[i] + w], mine, partner)
 
         def ff_piece(ref, at, w):
             have = min(w, ff - at)
@@ -287,32 +285,38 @@
                 send(("e1", i, j), W[i].at[g, p], W[i].at[g, p], dev_up[j])
 
         def e2(i):
+            dev_a, pa, dev_b, pb = way(gather[i][0], 0)
             for j in (1, 2, 3):
                 got(("e1", i, j), W[i].at[downs[j], p])
             send(("e2b", i), W[i].at[:, p], W[i].at[:, p], dev_b)
             send(("e2a", i), W[i].at[:, p], W[i].at[:, p], dev_a)
 
         def e3(i):
+            dev_a, pa, dev_b, pb = way(gather[i][0], 0)
             got(("e2a", i), W[i].at[:, pa])
             send(("e3", i), W[i].at[:, pa], W[i].at[:, pa], dev_b)
 
         def e4(i):
+            dev_a, pa, dev_b, pb = way(gather[i][0], 0)
             got(("e2b", i), W[i].at[:, pb])
             got(("e3", i), W[i].at[:, pab])
 
         iz = len(gather) - 1
 
         def z1():
+            dev_a, pa, dev_b, pb = way(gather[iz][0], 0)
             r = rows
             got(("e0", iz), W[iz].at[g, p, pl.ds(pl.multiple_of(r * o, r), r)])
             send(("e2b", iz), W[iz].at[g, p], W[iz].at[g, p], dev_b)
             send(("e2a", iz), W[iz].at[g, p], W[iz].at[g, p], dev_a)
 
         def z2():
+            dev_a, pa, dev_b, pb = way(gather[iz][0], 0)
             got(("e2a", iz), W[iz].at[g, pa])
             send(("e3", iz), W[iz].at[g, pa], W[iz].at[g, pa], dev_b)
 
         def z3():
+            dev_a, pa, dev_b, pb = way(gather[iz][0], 0)
             got(("e2b", iz), W[iz].at[g, pb])
             got(("e3", iz), W[iz].at[g, pab])
             for j in (1, 2, 3):
@@ -343,6 +347,7 @@
                 send(("z1", j), G[0].at[ups[j]], RZ.at[j - 1, :, :, 0:w], dev_up[j])
 
         def zf2():
+            dev_a, pa, dev_b, pb = way(reduce[0][0], 1)
             w = reduce[0][1]
             for j in (1, 2, 3):
                 got(("z1", j), RZ.at[j - 1, :, :, 0:w])
@@ -358,6 +363,7 @@
                 send(("z2", n), G[0].at[g, q], RY.at[n, :, 0:w], dev_b)
 
         def zf3():
+            dev_a, pa, dev_b, pb = way(reduce[0][0], 1)
             w = reduce[0][1]
             got(("z2", 0), RY.at[0, :, 0:w])
             G[0][g, pa] = G[0][g, pa] + RY[0, :, 0:w]
@@ -371,12 +377,14 @@
             finish_chunk(0, G[0][g, p].astype(F32) + RY[2, :, 0:w].astype(F32))
 
         def f1(i):
+            dev_a, pa, dev_b, pb = way(reduce[i][0], 1)
             w = reduce[i][1]
             k = i % RING
             for n, col in ((0, pab), (1, pb)):
                 send(("f1", k, n), G[i].at[:, col], R1.at[k, n, :, :, 0:w], dev_b)
 
         def f2(i):
+            dev_a, pa, dev_b, pb = way(reduce[i][0], 1)
             w = reduce[i][1]
             k = i % RING
             got(("f1", k, 0), R1.at[k, 0, :, :, 0:w])
@@ -386,6 +394,7 @@
             G[i][:, p] = G[i][:, p] + R1[k, 1, :, :, 0:w]
 
         def f3(i):
+            dev_a, pa, dev_b, pb = way(reduce[i][0], 1)
             w = reduce[i][1]
             k = i % RING
             got(("f2", k), R2.at[k, :, :, 0:w])
@@ -443,7 +452,7 @@
             def one(k):
                 at = pl.multiple_of(k * quarter, quarter)
                 dst[pl.ds(at, quarter), pl.ds(pl.multiple_of(b * block, block), block)] = (
-                    src[b, :, pl.ds(at, quarter)].astype(F32).T.astype(BF16)
+                    src[b, :, pl.ds(at, quarter)].T
                 )
 
             loop(4, one)
@@ -543,8 +552,25 @@
 
             lax.fori_loop(0, STATE_STEPS, step, 0)
 
+        def start_split(d, key, src, dst, to):
+            i = number(key)
+            for lo in range(0, STATE, SPLIT):
+                rr = pl.ds(lo, min(SPLIT, STATE - lo))
+                pltpu.make_async_remote_copy(
+                    src_ref=src.at[rr],
+                    dst_ref=dst.at[rr],
+                    send_sem=ss.at[i],
+                    recv_sem=rs.at[i],
+                    device_id=to,
+                    device_id_type=MESH,
+                ).start()
+            return d
+
+        def send_split(key, src, dst, to):
+            pending[key] = start_split(remote(key, src, dst, to), key, src, dst, to)
+
         def state_x(n):
-            send(("sx", n), ST.at[1 - x], SA.at[n], dev_x)
+            send_split(("sx", n), ST.at[1 - x], SA.at[n], dev_x)
 
         def near(n):
             return remote(("sz", n, 0), TZ, SZ.at[n, 0], away(n, 1))
@@ -584,7 +610,9 @@
                 TZ[r, :] = t.astype(BF16)
 
             state_rows(add)
-            pl.when(near_sends(n))(lambda: near(n).start())
+            pl.when(near_sends(n))(
+                lambda: start_split(near(n), ("sz", n, 0), TZ, SZ.at[n, 0], away(n, 1)) and None
+            )
 
         def state_far(n):
             if not doubling:
@@ -598,8 +626,8 @@
                     TY[r, :] = (TZ[r, :].astype(F32) + SZ[n, 0, r, :].astype(F32)).astype(BF16)
 
                 state_rows(add)
-                far(n, 1).start()
-                far(n, 2).start()
+                for j in (1, 2):
+                    start_split(far(n, j), ("sz", n, j), TY, SZ.at[n, 1], away(n, j))
 
         def state_end(n, dst):
             if doubling:
@@ -621,7 +649,7 @@
                 SB[r, :] = (total + jnp.where(firsts[n], mine, 0.0)).astype(BF16)
 
             state_rows(add)
-            send(("sy", n), SB, dst.at[x], dev_x)
+            send_split(("sy", n), SB, dst.at[x], dev_x)
 
         def state_got(n, dst):
             got(("sy", n), dst.at[1 - x])
@@ -671,8 +699,15 @@
                 tops.append(num / den)
             ATT[b, :, v_slice(hp)] = jnp.concatenate(tops, axis=0).T.astype(BF16)
 
-        def attention():
-            loop(2 * PAIRS, att_step)
+        def pairs(body, lo, n):
+            def step(i, z):
+                body(lo + i)
+                return z
+
+            lax.fori_loop(0, n, step, 0)
+
+        def attention(lo, n):
+            pairs(att_step, lo, n)
 
         def col(k):
             return pl.ds(pl.multiple_of(k * quarter, quarter), quarter)
@@ -698,12 +733,16 @@
             r2 = lax.rsqrt(jnp.mean(x1 * x1, axis=-1, keepdims=True) + EPS)
             NB[c, rr, :] = (x1 * r2 * GROW[1:2, :]).astype(BF16)
 
+        def proj_own():
+            out_proj(OWN, c)
+
         def second_norm():
-            out_proj(OWN, c)
             got("x1", RCV.at[0])
             loop(block // step_rows, norm_two)
             send("n2", NB.at[c], NB.at[c], partner)
             transpose_in(NB, N2T, c)
+
+        def second_norm_in():
             got("n2", NB.at[o])
             transpose_in(NB, N2T, o)
 
@@ -717,7 +756,7 @@
                 def one(r):
                     rr = pl.ds(pl.multiple_of(r * 64, 64), 64)
                     gate, up = TG[rr, 0:tw], TU[rr, 0:tw]
-                    sg = 1.0 / (1.0 + jnp.exp(-gate))
+                    sg = 0.5 + 0.5 * jnp.tanh(0.5 * gate)
                     silu = gate * sg
                     HID[rr, lo : lo + tw] = (silu * up).astype(BF16)
                     CA[rr, lo : lo + tw] = (up * sg * (1.0 + gate * (1.0 - sg))).astype(BF16)
@@ -757,6 +796,8 @@
             sent("x1")
             dn2(SND.at[0], o)
             send("dn2", SND.at[0], RCV.at[1], partner)
+
+        def dn2_own():
             dn2(OWN, c)
 
         def norm_two_back(r):
@@ -836,11 +877,7 @@
                 DQK[b, pl.ds(pl.multiple_of(QH + hp * 2 * FDIM + e * FDIM, FDIM), FDIM), :] = dk
 
         def back_rows(lo, n):
-            def step(i, z):
-                back_step(lo + i)
-                return z
-
-            lax.fori_loop(0, n, step, 0)
+            pairs(back_step, lo, n)
 
         def y_part(dst, b):
             def one(k):
@@ -859,6 +896,8 @@
         def y_send():
             y_part(SND.at[1], o)
             send("y", SND.at[1], RCV.at[2], partner)
+
+        def y_own():
             y_part(OWN, c)
 
         def y_end():
@@ -878,8 +917,10 @@
                 DQK[b, kr, :] += features_back(kk, df)
                 DV[b, hs, :] += nn(turned[VDIM * e : VDIM * (e + 1)], weighted(features(kk)))
 
-        def keys_back():
-            loop(2 * PAIRS, key_step)
+        def keys_back(lo, n):
+            pairs(key_step, lo, n)
+
+        def dqkv():
             for b in range(2):
                 DQKV[b, :, 0 : 2 * QH] = DQK[b].T.astype(BF16)
                 for at, tw in tiles_of(VH):
@@ -897,6 +938,8 @@
             sent("dn2")
             dn1(SND.at[0], o)
             send("dn1", SND.at[0], RCV.at[0], partner)
+
+        def dn1_own():
             dn1(OWN, c)
 
         def norm_one_back(r):
@@ -942,133 +985,194 @@
         def adv(st, name):
             go_to(st, ri[name])
 
+        def greeted():
+            pl.semaphore_wait(barrier, len(greet))
+            if members > 1:
+
+                @pl.when(hi < n_hi - 1)
+                def _():
+                    pl.semaphore_wait(barrier, 1)
+
+                @pl.when(hi > 0)
+                def _():
+                    pl.semaphore_wait(barrier, 1)
+
+        cx = local(tok, X.at[c])
+        cy = local(cot, DY.at[c])
         for i in range(len(gather)):
             e0(i)
+        cx.wait()
+        cy.wait()
+        greeted()
+
+        for i in range(len(gather)):
+            e0_send(i)
         send("x", X.at[c], X.at[c], partner)
         send("dy", DY.at[c], DY.at[c], partner)
         ga(1, 0)
-        gstep(-1)
-        gstep(0)
+        ga(1, 1)
+        ga(2, 0)
+        ga(1, 2)
+        ga(2, 1)
+        ga(3, 0)
         transpose_in(DY, DYT, c)
         got("x", X.at[o])
         got("dy", DY.at[o])
         transpose_in(DY, DYT, o)
-        gstep(1, 2, 1)
+        ga(1, 3)
+        ga(1, 4)
+        ga(2, 2)
+        ga(3, 1)
+        ga(4, 0)
         z1()
         gains()
         first_norm()
-        gstep(2, 2, 1)
+        ga(1, 5)
+        ga(2, 3)
+        ga(3, 2)
         ga(2, 4)
+        ga(4, 1)
         ga(4, 2)
         qkv()
         states()
         state_x(0)
-        gstep(3, 2, 1)
+        ga(1, 6)
+        ga(1, 7)
+        ga(1, 8)
+        ga(1, 9)
+        ga(1, 10)
+        ga(1, 11)
+        ga(2, 5)
+        ga(2, 6)
+        ga(3, 3)
+        state_z(0)
+        ga(2, 7)
+        ga(3, 4)
         z2()
-        gstep(4, 2, 1)
-        state_z(0)
-        gstep(5, 4, 1)
         state_far(0)
+        ga(2, 8)
+        ga(3, 5)
+        state_end(0, PB)
+        ga(2, 9)
+        ga(3, 6)
+        state_got(0, PB)
+        ga(3, 7)
         z3()
-        gstep(6, 5, 1)
-        state_end(0, PB)
-        gstep(7, 5, 1)
-        state_got(0, PB)
-        gstep(8, 5, 2)
-        attention()
-        gstep(9, 5, 2)
+        attention(0, 4)
+        attention(4, 4)
+        ga(2, 10)
+        ga(3, 8)
+        ga(4, 3)
         proj_send()
+        proj_own()
         second_norm()
-        gstep(10, 5, 2)
+        second_norm_in()
+        ga(2, 11)
+        ga(3, 9)
+        ga(4, 4)
+        ga(4, 5)
         ffn_in(0)
         grad("d0")
         zf1()
+        ga(3, 10)
+        ga(4, 6)
+        ga(4, 7)
         ffn_in(1)
         grad("d1")
-        adv(1, "d1")
+        go_to(1, 1)
         ga(3, 11)
+        ga(4, 8)
         ga(4, 9)
         ffn_in(2)
         grad("d2")
-        adv(1, "d2")
+        go_to(1, 2)
         z4()
         ffn_back(0)
-        adv(2, "d1")
+        go_to(2, 1)
         grad("g0")
-        adv(1, "g0")
+        go_to(1, 3)
         ga(4, 10)
         ffn_back(1)
-        adv(2, "d2")
-        adv(3, "d1")
+        go_to(2, 2)
+        go_to(3, 1)
+        grad("u0")
+        go_to(1, 4)
         ga(4, 11)
         ffn_back(2)
         dn2_send()
-        grad("u0")
-        adv(1, "u0")
+        go_to(2, 3)
+        dn2_own()
+        go_to(3, 2)
+        grad("g1")
+        go_to(1, 5)
         second_norm_back()
-        adv(4, "d1")
         datt()
+        go_to(2, 4)
         back_states()
         state_x(1)
-        grad("g1")
-        adv(2, "g0")
-        adv(3, "d2")
-        adv(1, "g1")
+        go_to(3, 3)
+        go_to(4, 1)
+        grad("u1")
+        go_to(4, 2)
+        go_to(1, 6)
         state_z(1)
+        go_to(2, 5)
+        go_to(3, 4)
         zf2()
-        adv(4, "d2")
-        grad("u1")
-        adv(2, "u0")
-        adv(3, "g0")
-        adv(1, "u1")
+        go_to(4, 3)
         back_rows(0, 4)
+        grad("g2")
+        go_to(1, 7)
         state_far(1)
-        grad("g2")
-        adv(2, "g1")
-        adv(3, "u0")
-        adv(4, "g0")
-        adv(1, "g2")
+        go_to(2, 6)
+        go_to(3, 5)
+        go_to(4, 4)
+        back_rows(4, 4)
+        grad("u2")
+        go_to(1, 8)
         zf3()
         state_end(1, PX)
-        back_rows(4, 4)
-        grad("u2")
-        adv(2, "u1")
-        adv(3, "g1")
-        adv(4, "u0")
-        adv(1, "u2")
+        go_to(2, 7)
+        go_to(3, 6)
+        go_to(4, 5)
+        grad("out")
+        go_to(1, 9)
+        y_send()
+        y_own()
         zf4()
-        y_send()
-        grad("out")
         state_got(1, PX)
-        keys_back()
+        keys_back(0, 4)
+        keys_back(4, 4)
+        dqkv()
         grad("qk")
-        adv(2, "g2")
-        adv(3, "u1")
-        adv(4, "g1")
-        adv(1, "out")
+        go_to(2, 8)
+        go_to(3, 7)
+        go_to(4, 6)
+        go_to(1, 10)
+        grad("v")
+        go_to(1, 11)
+        dn1_send()
         y_end()
-        adv(2, "u2")
-        adv(3, "g2")
-        adv(4, "u1")
-        adv(1, "qk")
-        grad("v")
-        adv(1, "v")
-        dn1_send()
-        adv(2, "out")
-        adv(3, "u2")
-        adv(4, "g2")
+        dn1_own()
+        go_to(2, 9)
+        go_to(3, 8)
+        go_to(4, 7)
         first_norm_back()
-        adv(1, "gain")
-        adv(2, "qk")
-        adv(3, "out")
-        adv(4, "u2")
-        adv(2, "v")
-        adv(3, "qk")
+        go_to(2, 10)
+        go_to(3, 9)
+        go_to(4, 8)
+        go_to(1, 12)
+        go_to(2, 11)
+        go_to(3, 10)
+        go_to(4, 9)
+        go_to(2, 12)
+        go_to(3, 11)
+        go_to(4, 10)
+        go_to(3, 12)
+        go_to(4, 11)
+        go_to(4, 12)
 
         n = len(reduce)
-        for k in range(n, n + 4):
-            for st in (1, 2, 3, 4):
-                go_to(st, min(n - 1, k - st))
         for i in range(n):
             got(("f4", i), go.at[o, :, offsets[i] : offsets[i] + reduce[i][1]])
         for d in local_pending:
@@ -1171,13 +1275,19 @@
     vmem_spec = pl.BlockSpec(memory_space=pltpu.VMEM)
     hbm_spec = pl.BlockSpec(memory_space=pltpu.HBM)
 
-    def kernel(o_in, i_in, g_hbm, o_out, i_out, ag, qg, kg, vg, og, fg, gg, ug, dg, g_in, sems):
+    def kernel(o_in, i_in, g_hbm, o_out, i_out, ag, qg, kg, vg, og, fg, gg, ug, dg, g_in, o_held, i_held, sems):
         c2 = pltpu.make_async_copy(g_hbm, g_in, sems.at[2])
         c2.start()
-        c0 = pltpu.make_async_copy(o_in, o_out, sems.at[0])
-        c1 = pltpu.make_async_copy(i_in, i_out, sems.at[1])
+        c0 = pltpu.make_async_copy(i_in, i_held, sems.at[0])
+        c1 = pltpu.make_async_copy(o_in, o_held, sems.at[1])
         c0.start()
         c1.start()
+        c0.wait()
+        c3 = pltpu.make_async_copy(i_held, i_out, sems.at[3])
+        c3.start()
+        c1.wait()
+        c4 = pltpu.make_async_copy(o_held, o_out, sems.at[4])
+        c4.start()
         c2.wait()
         gain = (g_in[0, :, at["gain"] : at["gain"] + LANES] + g_in[1, :, at["gain"] : at["gain"] + LANES]).T
         ag[...] = gain[0:1, :rows]
@@ -1193,8 +1303,8 @@
                 for ref, letter in ((gg, "g"), (ug, "u"), (dg, "d")):
                     a = at[f"{letter}{j}"]
                     ref[:, lo : lo + have] = g_in[h, :, a : a + have]
-        c0.wait()
-        c1.wait()
+        c3.wait()
+        c4.wait()
 
     shapes = [(1, rows), (rows, 2 * QH), (rows, 2 * QH), (rows, 2 * VH), (rows, 2 * VH), (1, rows)] + [(rows, ff)] * 3
     return pl.pallas_call(
@@ -1203,8 +1313,13 @@
         + [jax.ShapeDtypeStruct(n, F32) for n in shapes],
         in_specs=[hbm_spec] * 3,
         out_specs=[hbm_spec] * 2 + [vmem_spec] * len(shapes),
-        scratch_shapes=[pltpu.VMEM(grads.shape, F32), pltpu.SemaphoreType.DMA((3,))],
-        compiler_params=pltpu.CompilerParams(vmem_limit_bytes=32 * 2**20),
+        scratch_shapes=[
+            pltpu.VMEM(grads.shape, F32),
+            pltpu.VMEM(output.shape, BF16),
+            pltpu.VMEM(input_grad.shape, F32),
+            pltpu.SemaphoreType.DMA((5,)),
+        ],
+        compiler_params=pltpu.CompilerParams(vmem_limit_bytes=60 * 2**20),
     )(output, input_grad, grads)
 
 

time: 244 us -> 222 us (0.910)
  Pallas kernels: 239 us -> 220 us
  local copies, waits for them, and re-layouts: 3.62 us -> 0 us
    pallas_call x1, Pallas kernels: 236 us -> 216 us  [call_kernel(): pl.pallas_call(make_kernel(seq_size, block, width, ff, ff_half), out_shap...]
    unnamed x6 -> x0, local copies, waits for them, and re-layouts: 3.62 us -> none
where the time goes in v3:
time: 222 us; the launch traced here: 221 us
  Pallas kernels  220 us (99%)
    pallas_call x1, Pallas kernels, call_kernel(): pl.pallas_call(make_kernel(seq_size, block, width, ff, ff_half), out_shap...  216 us

profile of v3, /device:TPU:1, one launch (start us, length us, event | category | flops | bytes accessed | tf_op | source)
XLA Modules:
  0.0 220.7 jit_solution(18412650408531843689)
XLA Ops:
  0.6 215.9 %shard_map.194 = (bf16[256,1024]{1,0:T(8,128)(2,1)}, f32[256,1024]{1,0:T(8,128)}, f32[2,32,5632]{2,1,0:T(8,128)}) custom-call(bf16[256,1024]{1,0:T(8,128)(2,1)} %bitcast.12, bf16[256,1024]{1,0:T(8,128)(2,1)} %bitcast.13, bf16[1,32]{1,0:T(2,128)(2,1)} %bitcast.16, bf16[32,256]{1,0:T(8,128)(2,1)} %refs_3_.1, bf16[32,256]{1,0:T(8,128)(2,1)} %refs_4_.1, ...), custom_call_target="tpu_custom_call" | custom-call | tf_op jit(solution)/shard_map/pallas_call | solution.py:1253
  216.6 3.9 %shard_map.195 = (bf16[256,1024]{1,0:T(8,128)(2,1)}, f32[256,1024]{1,0:T(8,128)}, f32[1,32]{1,0:T(1,128)}, f32[32,256]{1,0:T(8,128)}, f32[32,256]{1,0:T(8,128)},...) custom-call(bf16[256,1024]{1,0:T(8,128)(2,1)} %get-tuple-element.25., ...), custom_call_target="tpu_custom_call" | custom-call | tf_op jit(solution)/shard_map/pallas_call | solution.py:1310

commit v4 on v3

--- a/solution.py
+++ b/solution.py
@@ -23,7 +23,7 @@
 STATE_STEPS = STATE // 16
 SPLIT = 96
 LANES = 128
-ALIKE = (("g0",), ())
+ALIKE = (("g0", "u2"), ())
 PIECE = 512
 RING = 6
 MESH = pl.DeviceIdType.MESH
@@ -201,7 +201,12 @@
         pending = {}
 
         def number(key):
-            return numbers.setdefault(key, len(numbers))
+            return numbers.setdefault(again(key), len(numbers))
+
+        def again(key):
+            if key[0] == "f1":
+                return (("e2b", key[1]), ("e3", key[1]))[key[2]]
+            return {"f2": ("e2a",), "f3": ("e1",), "f4": ("e0",)}.get(key[0], key[:1]) + key[1:]
 
         def remote(key, src, dst, to):
             i = number(key)
@@ -210,6 +215,7 @@
             )
 
         def send(key, src, dst, to):
+            key = again(key)
             if key in pending:
                 sent(key)
             d = remote(key, src, dst, to)
@@ -1009,12 +1015,14 @@
             e0_send(i)
         send("x", X.at[c], X.at[c], partner)
         send("dy", DY.at[c], DY.at[c], partner)
+        z1()
         ga(1, 0)
         ga(1, 1)
         ga(2, 0)
         ga(1, 2)
         ga(2, 1)
         ga(3, 0)
+        z2()
         transpose_in(DY, DYT, c)
         got("x", X.at[o])
         got("dy", DY.at[o])
@@ -1024,10 +1032,9 @@
         ga(2, 2)
         ga(3, 1)
         ga(4, 0)
-        z1()
+        ga(1, 5)
         gains()
         first_norm()
-        ga(1, 5)
         ga(2, 3)
         ga(3, 2)
         ga(2, 4)
@@ -1048,7 +1055,6 @@
         state_z(0)
         ga(2, 7)
         ga(3, 4)
-        z2()
         state_far(0)
         ga(2, 8)
         ga(3, 5)
@@ -1263,7 +1269,7 @@
 
 
 def n_messages(gather, reduce):
-    return 7 * len(gather) + 6 * RING + len(reduce) + 24
+    return 7 * len(gather) + 24
 
 
 def call_finish(output, input_grad, grads, ff, ff_half):

time: 222 us -> 219 us (0.986)
  Pallas kernels: 220 us -> 217 us
    pallas_call x1, Pallas kernels: 216 us -> 213 us  [call_kernel(): pl.pallas_call(make_kernel(seq_size, block, width, ff, ff_half), out_shap...]
where the time goes in v4:
time: 219 us; the launch traced here: 218 us
  Pallas kernels  217 us (99%)
    pallas_call x1, Pallas kernels, call_kernel(): pl.pallas_call(make_kernel(seq_size, block, width, ff, ff_half), out_shap...  213 us

profile of v4, /device:TPU:1, one launch (start us, length us, event | category | flops | bytes accessed | tf_op | source)
XLA Modules:
  0.0 217.7 jit_solution(14702423338377465098)
XLA Ops:
  0.6 213.0 %shard_map.194 = (bf16[256,1024]{1,0:T(8,128)(2,1)}, f32[256,1024]{1,0:T(8,128)}, f32[2,32,5632]{2,1,0:T(8,128)}) custom-call(bf16[256,1024]{1,0:T(8,128)(2,1)} %bitcast.12, bf16[256,1024]{1,0:T(8,128)(2,1)} %bitcast.13, bf16[1,32]{1,0:T(2,128)(2,1)} %bitcast.16, bf16[32,256]{1,0:T(8,128)(2,1)} %refs_3_.1, bf16[32,256]{1,0:T(8,128)(2,1)} %refs_4_.1, ...), custom_call_target="tpu_custom_call" | custom-call | tf_op jit(solution)/shard_map/pallas_call | solution.py:1259
  213.7 3.9 %shard_map.195 = (bf16[256,1024]{1,0:T(8,128)(2,1)}, f32[256,1024]{1,0:T(8,128)}, f32[1,32]{1,0:T(1,128)}, f32[32,256]{1,0:T(8,128)}, f32[32,256]{1,0:T(8,128)},...) custom-call(bf16[256,1024]{1,0:T(8,128)(2,1)} %get-tuple-element.25., ...), custom_call_target="tpu_custom_call" | custom-call | tf_op jit(solution)/shard_map/pallas_call | solution.py:1316

commit v5 on v4

--- a/solution.py
+++ b/solution.py
@@ -1033,6 +1033,7 @@
         ga(3, 1)
         ga(4, 0)
         ga(1, 5)
+        ga(1, 6)
         gains()
         first_norm()
         ga(2, 3)
@@ -1043,7 +1044,6 @@
         qkv()
         states()
         state_x(0)
-        ga(1, 6)
         ga(1, 7)
         ga(1, 8)
         ga(1, 9)
@@ -1155,19 +1155,19 @@
         go_to(3, 7)
         go_to(4, 6)
         go_to(1, 10)
+        y_end()
+        dn1_send()
         grad("v")
         go_to(1, 11)
-        dn1_send()
-        y_end()
         dn1_own()
         go_to(2, 9)
         go_to(3, 8)
         go_to(4, 7)
         first_norm_back()
+        go_to(1, 12)
         go_to(2, 10)
         go_to(3, 9)
         go_to(4, 8)
-        go_to(1, 12)
         go_to(2, 11)
         go_to(3, 10)
         go_to(4, 9)

time: 219 us -> 219 us (level)
  no operation moved by 1% of the time
where the time goes in v5:
time: 219 us
  Pallas kernels  218 us (100%)
    pallas_call x1, Pallas kernels, call_kernel(): pl.pallas_call(make_kernel(seq_size, block, width, ff, ff_half), out_shap...  215 us

profile of v5, /device:TPU:1, one launch (start us, length us, event | category | flops | bytes accessed | tf_op | source)
XLA Modules:
  0.0 219.3 jit_solution(9190889424897418756)
XLA Ops:
  0.6 214.5 %shard_map.194 = (bf16[256,1024]{1,0:T(8,128)(2,1)}, f32[256,1024]{1,0:T(8,128)}, f32[2,32,5632]{2,1,0:T(8,128)}) custom-call(bf16[256,1024]{1,0:T(8,128)(2,1)} %bitcast.12, bf16[256,1024]{1,0:T(8,128)(2,1)} %bitcast.13, bf16[1,32]{1,0:T(2,128)(2,1)} %bitcast.16, bf16[32,256]{1,0:T(8,128)(2,1)} %refs_3_.1, bf16[32,256]{1,0:T(8,128)(2,1)} %refs_4_.1, ...), custom_call_target="tpu_custom_call" | custom-call | tf_op jit(solution)/shard_map/pallas_call | solution.py:1259
  215.2 3.9 %shard_map.195 = (bf16[256,1024]{1,0:T(8,128)(2,1)}, f32[256,1024]{1,0:T(8,128)}, f32[1,32]{1,0:T(1,128)}, f32[32,256]{1,0:T(8,128)}, f32[32,256]{1,0:T(8,128)},...) custom-call(bf16[256,1024]{1,0:T(8,128)(2,1)} %get-tuple-element.25., ...), custom_call_target="tpu_custom_call" | custom-call | tf_op jit(solution)/shard_map/pallas_call | solution.py:1316
